TPU v7x, 256 devices: a whole 4x4x8 slice. The times are simulated.
256 devices in a mesh: pb: 32 (over z, y_hi, core), ka: 8 (over x, y_lo).
Axes of the slice: x: 4, y: 4 (y_hi: 2, y_lo: 2; y = y_hi * 2 + y_lo), z: 8, core: 2. Of those that a mesh axis runs over, the one named last changes fastest.
Arguments:
- queries: bfloat16 [32768, 128], P(('pb', 'ka')), may hold values from -4 to 4
- key_rows: bfloat16 [32768, 128], P(('pb', 'ka')), may hold values from -4 to 4
- value_rows: bfloat16 [32768, 128], P(('pb', 'ka')), may hold values from -6 to 6
- outputs: bfloat16 [32768, 128], P(('pb', 'ka')), may hold values from -3 to 3
- out_grad: bfloat16 [32768, 128], P(('pb', 'ka')), may hold values from -6 to 6
- log_sums: float32 [32768], P(('pb', 'ka')), may hold values from 3 to 6
- doc_lengths: int32 [16], replicated, may hold values from 1 to 24576, 32768 in all
- tile_allowed: int32 [16, 16], replicated, may hold values from 0 to 1, as said below
Outputs:
- query_grad: bfloat16 [32768, 128], P(('pb', 'ka'))
- key_grad: bfloat16 [32768, 128], P(('pb', 'ka'))
- value_grad: bfloat16 [32768, 128], P(('pb', 'ka'))
Inputs may be any that keep to these rules, and one draw needn't show every extreme that they name: tile_allowed is 1 on the diagonal and 0 above it.
All inputs are finite; a program needn't handle non-finite values.
Results may differ from a plain program's by a relative error of at most 0.02.
Values may be sent and summed in bfloat16 or wider, within the bound.
No kernel may reach another device: no remote copies, remote signals or barrier semaphores. Data moves between devices by JAX's collectives and lax.ppermute only.
A program may use at most 64 MiB of HBM per device.

v0:
```python
import jax
import jax.numpy as jnp
from jax import lax
from jax.sharding import PartitionSpec as P

TILE = 2048


def document_of(positions, doc_ends):
    return jnp.sum((positions[:, None] >= doc_ends[None, :]).astype(jnp.int32), axis=1)


def tile_grads(q_part, g_part, lse_part, delta_part, key_block, value_block, visible, score_scale):
    scores = jnp.dot(q_part, key_block.T, preferred_element_type=jnp.float32) * score_scale
    probs = jnp.where(visible, jnp.exp(scores - lse_part[:, None]), jnp.float32(0.0))
    probs_low = probs.astype(jnp.bfloat16)
    value_part = jnp.dot(probs_low.T, g_part, preferred_element_type=jnp.float32)
    prob_grad = jnp.dot(g_part, value_block.T, preferred_element_type=jnp.float32)
    score_grad = (probs * (prob_grad - delta_part[:, None])).astype(jnp.bfloat16)
    query_part = jnp.dot(score_grad, key_block, preferred_element_type=jnp.float32)
    key_part = jnp.dot(score_grad.T, q_part, preferred_element_type=jnp.float32)
    return (query_part, key_part, value_part)


def on_device(
    queries, key_rows, value_rows, outputs, out_grad, log_sums, doc_lengths, tile_allowed
):
    width = queries.shape[1]
    score_scale = width ** (-0.5)
    local_rows = key_rows.shape[0]
    row_delta = jnp.sum(out_grad.astype(jnp.float32) * outputs.astype(jnp.float32), axis=1)
    q_all, g_all = (
        lax.all_gather(queries, "ka", axis=0, tiled=True),
        lax.all_gather(out_grad, "ka", axis=0, tiled=True),
    )
    lse_all, delta_all = (
        lax.all_gather(log_sums, "ka", axis=0, tiled=True),
        lax.all_gather(row_delta, "ka", axis=0, tiled=True),
    )
    k_all, v_all = (
        lax.all_gather(key_rows, "pb", axis=0, tiled=True),
        lax.all_gather(value_rows, "pb", axis=0, tiled=True),
    )
    qblock = q_all.shape[0]
    half_rows = qblock // 2
    kblock = k_all.shape[0]
    pb_index = lax.axis_index("pb")
    ka_index = lax.axis_index("ka")
    stride = local_rows * lax.axis_size("ka")
    q_start = pb_index * qblock
    half_range = jnp.arange(half_rows, dtype=jnp.int32)
    lower_pos = q_start + half_range
    upper_rows = (q_all[half_rows:], g_all[half_rows:])
    upper_stats = (lse_all[half_rows:], delta_all[half_rows:])
    upper_pos = q_start + half_rows + half_range
    query_parts = [
        (
            q_all[:half_rows],
            g_all[:half_rows],
            lse_all[:half_rows],
            delta_all[:half_rows],
            lower_pos,
        ),
        (upper_rows[0], upper_rows[1], upper_stats[0], upper_stats[1], upper_pos),
    ]
    doc_ends = jnp.cumsum(doc_lengths)
    tile_count = tile_allowed.shape[0]
    allowed = tile_allowed.astype(jnp.float32)
    tile_ids = jnp.arange(tile_count, dtype=jnp.int32)
    prepared = []
    for q_part, g_part, lse_part, delta_part, positions in query_parts:
        doc_ids = document_of(positions, doc_ends)
        row_tiles = (positions[:, None] // TILE == tile_ids[None, :]).astype(jnp.float32)
        rows_ok = jnp.dot(row_tiles, allowed, precision=lax.Precision.HIGHEST)
        prepared.append((q_part, g_part, lse_part, delta_part, positions, doc_ids, rows_ok))
    key_width = min(kblock, 1024)
    key_count = kblock // key_width
    key_blocks = k_all.reshape(key_count, key_width, width)
    value_blocks = v_all.reshape(key_count, key_width, width)

    def key_step(dq_carry, inputs):
        key_block, value_block, index = inputs
        gathered_row = index * key_width + jnp.arange(key_width, dtype=jnp.int32)
        key_pos = (
            gathered_row // local_rows * stride + ka_index * local_rows + gathered_row % local_rows
        )
        key_docs = document_of(key_pos, doc_ends)
        key_tiles = (key_pos[:, None] // TILE == tile_ids[None, :]).astype(jnp.float32)
        key_sum = jnp.zeros((key_width, width), jnp.float32)
        value_sum = jnp.zeros((key_width, width), jnp.float32)
        new_carry = []
        for number in range(2):
            q_part, g_part, lse_part, delta_part, positions, doc_ids, rows_ok = prepared[number]
            tile_ok = jnp.dot(rows_ok, key_tiles.T, precision=lax.Precision.HIGHEST) > 0.5
            visible = (
                (positions[:, None] >= key_pos[None, :])
                & (doc_ids[:, None] == key_docs[None, :])
                & tile_ok
            )

            def active():
                return tile_grads(
                    q_part,
                    g_part,
                    lse_part,
                    delta_part,
                    key_block,
                    value_block,
                    visible,
                    score_scale,
                )

            def passive():
                return (
                    jnp.zeros((half_rows, width), jnp.float32),
                    jnp.zeros((key_width, width), jnp.float32),
                    jnp.zeros((key_width, width), jnp.float32),
                )

            query_part, key_part, value_part = lax.cond(jnp.any(visible), active, passive)
            new_carry.append(dq_carry[number] + query_part)
            key_sum = key_sum + key_part
            value_sum = value_sum + value_part
        return ((new_carry[0], new_carry[1]), (key_sum, value_sum))

    start_carry = (
        jnp.zeros((half_rows, width), jnp.float32),
        jnp.zeros((half_rows, width), jnp.float32),
    )
    (dq_lower, dq_upper), (key_terms, value_terms) = lax.scan(
        key_step, start_carry, (key_blocks, value_blocks, jnp.arange(key_count, dtype=jnp.int32))
    )
    dq_terms = jnp.concatenate([dq_lower, dq_upper], axis=0)
    query_sum = lax.psum_scatter(dq_terms, "ka", scatter_dimension=0, tiled=True)
    key_sum, value_sum = (
        lax.psum_scatter(
            key_terms.reshape(kblock, width).astype(jnp.bfloat16),
            "pb",
            scatter_dimension=0,
            tiled=True,
        ).astype(jnp.float32),
        lax.psum_scatter(
            value_terms.reshape(kblock, width).astype(jnp.bfloat16),
            "pb",
            scatter_dimension=0,
            tiled=True,
        ).astype(jnp.float32),
    )
    query_grad = (query_sum * score_scale).astype(jnp.bfloat16)
    key_grad = (key_sum * score_scale).astype(jnp.bfloat16)
    value_grad = value_sum.astype(jnp.bfloat16)
    return (query_grad, key_grad, value_grad)


def solution(mesh):
    in_specs = (
        P(("pb", "ka"), None),
        P(("pb", "ka"), None),
        P(("pb", "ka"), None),
        P(("pb", "ka"), None),
        P(("pb", "ka"), None),
        P(("pb", "ka")),
        P(),
        P(),
    )
    out_specs = (P(("pb", "ka"), None), P(("pb", "ka"), None), P(("pb", "ka"), None))
    return jax.shard_map(
        on_device, mesh=mesh, in_specs=in_specs, out_specs=out_specs, check_vma=False
    )
```

profile of v0, /device:TPU:32, one launch (start us, length us, event | category | flops | bytes accessed | tf_op | source)
XLA Modules:
  0.0 528.2 jit_solution(2458604532467396944)
XLA Ops:
  7.2 0.7 all-gather.5.cloned.1.call-update
  7.9 0.7 all-gather.7.cloned.1.call-update
  8.7 0.9 multiply_reduce_fusion
  9.6 18.7 %all-gather.1 = f32[8,1,128]{2,1,0:T(1,128)S(1)} all-gather(f32[1,1,128]{2,1,0:T(1,128)S(1)} %bitcast.64), channel_id=1, replica_groups=mesh['pb'=32,'ka'=8] {'ka'}, dimensions={0}, use_global_device_ids=true | all-gather | bytes 4608 | tf_op jit(solution)/shard_map/all_gather | solution.py:38
  28.4 15.2 %all-gather = f32[8,1,128]{2,1,0:T(1,128)S(1)} all-gather(f32[1,1,128]{2,1,0:T(1,128)} %bitcast.65), channel_id=1, replica_groups=mesh['pb'=32,'ka'=8] {'ka'}, dimensions={0}, use_global_device_ids=true | all-gather | bytes 4608 | tf_op jit(solution)/shard_map/all_gather | solution.py:37
  43.6 0.7 copy.22
  44.6 28.7 %all_gather.22 = bf16[1024,128]{1,0:T(8,128)(2,1)S(1)} all-gather(bf16[128,128]{1,0:T(8,128)(2,1)} %param.18), channel_id=1, replica_groups=mesh['pb'=32,'ka'=8] {'ka'}, dimensions={0}, use_global_device_ids=true | all-gather | bytes 294912 | tf_op jit(solution)/shard_map/all_gather | solution.py:34
  73.3 28.7 %all_gather.20 = bf16[1024,128]{1,0:T(8,128)(2,1)S(1)} all-gather(bf16[128,128]{1,0:T(8,128)(2,1)} %param.14), channel_id=1, replica_groups=mesh['pb'=32,'ka'=8] {'ka'}, dimensions={0}, use_global_device_ids=true | all-gather | bytes 294912 | tf_op jit(solution)/shard_map/all_gather | solution.py:33
  102.0 1.0 fusion.22
  103.0 1.0 fusion.23
  104.2 63.0 %all-gather.7.cloned.1.call-done = bf16[4096,128]{1,0:T(8,128)(2,1)} async-done(((bf16[128,128]{1,0:T(8,128)(2,1)}), bf16[4096,128]{1,0:T(8,128)(2,1)}) %all-gather.7.cloned.1.call-update) | async-done | bytes 1048592 | tf_op jit(solution)/shard_map/all_gather | solution.py:42
  167.2 59.5 %while.20 = (s32[]{:T(128)}, f32[512,128]{1,0:T(8,128)}, f32[512,128]{1,0:T(8,128)S(1)}, bf16[4,1024,128]{2,1,0:T(8,128)(2,1)}, bf16[4,1024,128]{2,1,0:T(8,128)(...) while((s32[]{:T(128)}, f32[512,128]{1,0:T(8,128)}, ...), condition=%wide.region_12.13_spmd.clone, body=%wide.region_4.12_spmd.clone.sunk | while | flops 1557804032 | bytes 34206244 | solution.py:130
  167.2 0.6 dynamic_slice.33
  168.5 1.0 dynamic-slice_bitcast_fusion.5
  169.5 1.0 dynamic-slice_bitcast_fusion.4
  170.5 3.3 fusion.73
  174.4 2.6 fusion.72
  177.5 3.1 conditional.6
  177.5 0.6 copy.21
  178.2 0.6 exponential_select_fusion.1
  178.8 0.5 fusion.8
  179.3 0.4 multiply_convert_fusion.1
  179.7 0.4 fusion.42
  180.2 0.5 fusion.43
  180.7 4.2 conditional.7
  180.7 1.7 copy.20
  182.4 0.7 exponential_select_fusion
  183.1 0.5 fusion.6
  183.5 0.4 multiply_convert_fusion
  184.0 0.4 fusion.40
  184.4 0.5 fusion.41
  184.9 0.9 select_add_fusion.3
  185.8 0.9 bitcast_dynamic-update-slice_fusion.3
  186.7 0.6 dynamic_slice.33
  188.1 1.0 dynamic-slice_bitcast_fusion.5
  189.0 1.0 dynamic-slice_bitcast_fusion.4
  190.0 3.3 fusion.73
  193.9 2.6 fusion.72
  197.2 0.1 conditional.7
  197.3 1.8 select_add_fusion.3
  199.1 0.9 bitcast_dynamic-update-slice_fusion.3
  200.0 0.6 dynamic_slice.33
  201.4 1.0 dynamic-slice_bitcast_fusion.5
  202.4 1.0 dynamic-slice_bitcast_fusion.4
  203.4 3.3 fusion.73
  207.2 2.6 fusion.72
  210.5 0.1 conditional.7
  210.7 1.8 select_add_fusion.3
  212.5 0.9 bitcast_dynamic-update-slice_fusion.3
  213.4 0.6 dynamic_slice.33
  214.7 1.0 dynamic-slice_bitcast_fusion.5
  215.7 1.0 dynamic-slice_bitcast_fusion.4
  216.7 3.3 fusion.73
  220.5 2.6 fusion.72
  224.0 1.8 select_add_fusion.3
  225.8 0.9 bitcast_dynamic-update-slice_fusion.3
  226.7 1.8 pad_maximum_fusion
  228.5 0.5 reduce-scatter.6.cloned.1.call-update
  229.1 0.5 reduce-scatter.8.cloned.1.call-update
  229.7 56.7 %reduce-scatter.4.cloned.1.call-done = f32[128,128]{1,0:T(8,128)} async-done(((f32[1024,128]{1,0:T(8,128)}), f32[128,128]{1,0:T(8,128)}) %reduce-scatter.4.cloned.1.call-update) | async-done | bytes 65552 | tf_op jit(solution)/shard_map/reduce_scatter | solution.py:134
  286.3 1.5 multiply_convert_fusion.3
  287.8 116.0 %reduce-scatter.6.cloned.1.call-done = bf16[128,128]{1,0:T(8,128)(2,1)} async-done(((bf16[4096,128]{1,0:T(8,128)(2,1)}), bf16[128,128]{1,0:T(8,128)(2,1)}) %reduce-scatter.6.cloned.1.call-update) | async-done | bytes 32784 | tf_op jit(solution)/shard_map/reduce_scatter | solution.py:136
  403.8 1.4 multiply_convert_fusion.2
  405.2 116.5 %reduce-scatter.8.cloned.1.call-done = bf16[128,128]{1,0:T(8,128)(2,1)} async-done(((bf16[4096,128]{1,0:T(8,128)(2,1)}), bf16[128,128]{1,0:T(8,128)(2,1)}) %reduce-scatter.8.cloned.1.call-update) | async-done | bytes 32784 | tf_op jit(solution)/shard_map/reduce_scatter | solution.py:142
  (64 shorter events, 2.2 us)
Async XLA Ops:
  7.2 97.0 %all-gather.5.cloned.1.call-start = ((), (), s32[]{:S(2)}) async-start(), calls=%async_computation.3 | async-start | bytes 1081344 | tf_op jit(solution)/shard_map/all_gather | solution.py:41
  7.9 159.3 %all-gather.7.cloned.1.call-start = ((), (), s32[]{:S(2)}) async-start(), calls=%async_computation.4 | async-start | bytes 1081344 | tf_op jit(solution)/shard_map/all_gather | solution.py:42
  8.6 277.7 %reduce-scatter.4.cloned.1.call-start = ((), (), s32[]{:S(2)}) async-start(), calls=%async_computation.5 | async-start | bytes 589824 | tf_op jit(solution)/shard_map/reduce_scatter | solution.py:134
  228.5 175.3 %reduce-scatter.6.cloned.1.call-start = ((), (), s32[]{:S(2)}) async-start(), calls=%async_computation.6 | async-start | bytes 1081344 | tf_op jit(solution)/shard_map/reduce_scatter | solution.py:136
  229.1 292.5 %reduce-scatter.8.cloned.1.call-start = ((), (), s32[]{:S(2)}) async-start(), calls=%async_computation.7 | async-start | bytes 1081344 | tf_op jit(solution)/shard_map/reduce_scatter | solution.py:142
Sparse Core Ops, SparseCore 0:
  10.8 79.5 all-gather.4
  93.2 73.9 all-gather.6
  228.6 57.6 reduce-scatter.3
  290.8 112.9 reduce-scatter.5
  408.3 113.3 reduce-scatter.7
where the time goes:
time: 530 us; the launch traced here: 528 us
  waiting for transfers between devices  355 us (67%)
  blocking collectives  91.4 us (17%)
  matrix products  30.5 us (6%)
  other arithmetic  16.2 us (3%)
  between operations  13.9 us (3%)
  local copies, waits for them, and re-layouts  13.8 us (3%)
  loops' own time  7.54 us (1%)
    reduce_scatter x1, waiting for transfers between devices, on_device(): lax.psum_scatter(value_terms.reshape(kblock, width).astype(jnp.bfloat16),...  116 us
    reduce_scatter x1, waiting for transfers between devices, on_device(): lax.psum_scatter(key_terms.reshape(kblock, width).astype(jnp.bfloat16), '...  116 us
    all_gather x1, waiting for transfers between devices, on_device(): lax.all_gather(value_rows, 'pb', axis=0, tiled=True)  63 us
    reduce_scatter x1, waiting for transfers between devices, on_device(): lax.psum_scatter(dq_terms, 'ka', scatter_dimension=0, tiled=True)  56.7 us
    all_gather x1, blocking collectives, on_device(): lax.all_gather(out_grad, 'ka', axis=0, tiled=True)  28.7 us
    all_gather x1, blocking collectives, on_device(): lax.all_gather(queries, 'ka', axis=0, tiled=True)  28.7 us
    dot_general x8, matrix products, key_step(): jnp.dot(rows_ok, key_tiles.T, precision=lax.Precision.HIGHEST) > 0.5  23.5 us
    all_gather x1, blocking collectives, on_device(): lax.all_gather(row_delta, 'ka', axis=0, tiled=True)  18.7 us
  transfers between devices with their start and end apart: 5, of which 4 were waited for; matrix products, arithmetic and copies ran while one was open for 1% of the time, Pallas kernels for 0%

commit v1 on v0

v1 whole, which is shorter than its diff:
```python
import functools
import math

import jax
import jax.numpy as jnp
from jax import lax
from jax.experimental import pallas as pl
from jax.experimental.pallas import tpu as pltpu
from jax.sharding import Mesh, PartitionSpec as P

AXES = ("z", "yh", "c", "x", "yl")
SIZES = (8, 2, 2, 4, 2)
ROWS = 128
WIDTH = 128
NDOCS = 16
TILE = 2048
RUN = 1024
CHUNK = 256
PACK = 272
LOG2E = math.log2(math.e)
SCALE = 128.0 ** -0.5


def split3(x):
    a = x.astype(jnp.bfloat16)
    r = x - a.astype(jnp.float32)
    b = r.astype(jnp.bfloat16)
    c = (r - b.astype(jnp.float32)).astype(jnp.bfloat16)
    return a, b, c


def pack_kernel(q_ref, g_ref, o_ref, lse_ref, out_ref):
    prod = g_ref[...].astype(jnp.float32) * o_ref[...].astype(jnp.float32)
    delta = jnp.sum(prod.T, axis=0, keepdims=True)
    lse2 = lse_ref[...] * LOG2E
    out_ref[0:128] = q_ref[...]
    out_ref[128:256] = g_ref[...]
    parts = split3(lse2) + split3(delta)
    stats = jnp.concatenate(
        [p.astype(jnp.float32) for p in parts] + [jnp.zeros((10, ROWS), jnp.float32)], axis=0
    )
    out_ref[256:272] = stats.astype(jnp.bfloat16)


def pack(q, g, o, lse):
    return pl.pallas_call(
        pack_kernel,
        out_shape=jax.ShapeDtypeStruct((PACK, WIDTH), jnp.bfloat16),
    )(q, g, o, lse)


def grad_kernel(
    where_ref, len_ref, allow_ref, own_ref, other_ref, kv_ref,
    dqo_ref, dqx_ref, dkv_ref, kt_ref, dk_acc, dv_acc, dqt_acc,
):
    z, yh, c, qoff = where_ref[0], where_ref[1], where_ref[2], where_ref[3]
    ends = []
    total = jnp.int32(0)
    for d in range(NDOCS):
        total = total + len_ref[d]
        ends.append(total)
    for r in range(2):
        k_run = kv_ref[8 * r : 8 * r + 8, 0:128, :].reshape(RUN, WIDTH)
        kt_ref[r] = k_run.T
    dk_acc[...] = jnp.zeros_like(dk_acc)
    dv_acc[...] = jnp.zeros_like(dv_acc)
    dqt_acc[...] = jnp.zeros_like(dqt_acc)

    def first_start(pos):
        s = jnp.int32(0)
        for e in ends:
            s = jnp.where(e <= pos, e, s)
        return s

    lane = lax.broadcasted_iota(jnp.int32, (1, 2 * ROWS), 1)

    def q_step(zq, carry):
        base = zq * (2 * TILE) + yh * TILE + qoff
        p_own = base + c * RUN
        p_other = base + (1 - c) * RUN
        s_own = first_start(p_own)
        s_other = first_start(p_other)
        pos = jnp.where(lane < ROWS, p_own + lane, p_other - ROWS + lane)
        start = jnp.zeros_like(pos)
        for e in ends:
            start = jnp.where(pos >= e, e, start)

        for r in range(2):
            b = z * (2 * TILE) + r * TILE + c * RUN
            ok = allow_ref[2 * zq + yh, 2 * z + r] == 1
            live_own = (s_own <= b + RUN - 1) & (b <= p_own + ROWS - 1)
            live_other = (s_other <= b + RUN - 1) & (b <= p_other + ROWS - 1)

            @pl.when(ok & (live_own | live_other))
            def _unit():
                q = jnp.concatenate([own_ref[zq, 0:128], other_ref[zq, 0:128]], axis=0)
                g = jnp.concatenate([own_ref[zq, 128:256], other_ref[zq, 128:256]], axis=0)
                st = jnp.concatenate(
                    [own_ref[zq, 256:272], other_ref[zq, 256:272]], axis=1
                ).astype(jnp.float32)
                lse2 = st[0:1] + st[1:2] + st[2:3]
                delta = st[3:4] + st[4:5] + st[5:6]
                dqt = dqt_acc[zq]
                for n in range(RUN // CHUNK):
                    blk = 8 * r + 2 * n
                    k = kv_ref[blk : blk + 2, 0:128, :].reshape(CHUNK, WIDTH)
                    v = kv_ref[blk : blk + 2, 128:256, :].reshape(CHUNK, WIDTH)
                    st_ = lax.dot_general(
                        k, q, (((1,), (1,)), ((), ())), preferred_element_type=jnp.float32
                    )
                    dp = lax.dot_general(
                        v, g, (((1,), (1,)), ((), ())), preferred_element_type=jnp.float32
                    )
                    key = (b + n * CHUNK) + lax.broadcasted_iota(
                        jnp.int32, (CHUNK, 2 * ROWS), 0
                    )
                    vis = (key >= start) & (key <= pos)
                    p = jnp.where(vis, jnp.exp2(st_ * (SCALE * LOG2E) - lse2), 0.0)
                    pb = p.astype(jnp.bfloat16)
                    ds = (p * (dp - delta)).astype(jnp.bfloat16)
                    rows = pl.ds(r * RUN + n * CHUNK, CHUNK)
                    dv_acc[rows] += jnp.dot(pb, g, preferred_element_type=jnp.float32)
                    dk_acc[rows] += jnp.dot(ds, q, preferred_element_type=jnp.float32)
                    dqt = dqt + jnp.dot(
                        kt_ref[r, :, n * CHUNK : (n + 1) * CHUNK],
                        ds,
                        preferred_element_type=jnp.float32,
                    )
                dqt_acc[zq] = dqt

        return carry

    lax.fori_loop(z, 8, q_step, 0)
    for zq in range(8):
        dq = dqt_acc[zq].T.astype(jnp.bfloat16)
        dqo_ref[zq] = dq[0:128]
        dqx_ref[zq] = dq[128:256]
    for blk in range(16):
        dkv_ref[blk, 0:128] = dk_acc[blk * ROWS : (blk + 1) * ROWS].astype(jnp.bfloat16)
        dkv_ref[blk, 128:256] = dv_acc[blk * ROWS : (blk + 1) * ROWS].astype(jnp.bfloat16)


def grads(where, doc_lengths, tile_allowed, own, other, kv):
    smem = pl.BlockSpec(memory_space=pltpu.SMEM)
    vmem = pl.BlockSpec(memory_space=pltpu.VMEM)
    bf = jnp.bfloat16
    return pl.pallas_call(
        grad_kernel,
        out_shape=(
            jax.ShapeDtypeStruct((8, ROWS, WIDTH), bf),
            jax.ShapeDtypeStruct((8, ROWS, WIDTH), bf),
            jax.ShapeDtypeStruct((16, 2 * ROWS, WIDTH), bf),
        ),
        in_specs=[smem, smem, smem, vmem, vmem, vmem],
        out_specs=(vmem, vmem, vmem),
        scratch_shapes=[
            pltpu.VMEM((2, WIDTH, RUN), bf),
            pltpu.VMEM((2 * RUN, WIDTH), jnp.float32),
            pltpu.VMEM((2 * RUN, WIDTH), jnp.float32),
            pltpu.VMEM((8, WIDTH, 2 * ROWS), jnp.float32),
        ],
        compiler_params=pltpu.CompilerParams(vmem_limit_bytes=32 * 1024 * 1024),
    )(where, doc_lengths, tile_allowed, own, other, kv)


def on_device(
    queries, key_rows, value_rows, outputs, out_grad, log_sums, doc_lengths, tile_allowed
):
    z, yh, c = lax.axis_index("z"), lax.axis_index("yh"), lax.axis_index("c")
    qoff = (lax.axis_index("x") * 2 + lax.axis_index("yl")) * ROWS
    where = jnp.stack([z, yh, c, qoff]).astype(jnp.int32)
    plane = ("yh", "x", "yl")
    swap = [(0, 1), (1, 0)]

    kv = jnp.concatenate([key_rows, value_rows], axis=0)
    kv_all = lax.all_to_all(
        jnp.broadcast_to(kv[None], (16, 2 * ROWS, WIDTH)), plane, 0, 0, tiled=True
    )
    qg = pack(queries, out_grad, outputs, log_sums.reshape(1, ROWS))
    own = lax.all_to_all(jnp.broadcast_to(qg[None], (8, PACK, WIDTH)), "z", 0, 0, tiled=True)
    other = lax.ppermute(own, "c", swap)
    dq_own, dq_other, dkv = grads(where, doc_lengths, tile_allowed, own, other, kv_all)
    dq_in = lax.ppermute(dq_other, "c", swap)
    dkv_in = lax.all_to_all(dkv, plane, 0, 0, tiled=True)
    dq_pair = (dq_own.astype(jnp.float32) + dq_in.astype(jnp.float32)).astype(jnp.bfloat16)
    dq_all = lax.all_to_all(dq_pair, "z", 0, 0, tiled=True)
    query_grad = (jnp.sum(dq_all.astype(jnp.float32), axis=0) * SCALE).astype(jnp.bfloat16)
    dkv_sum = jnp.sum(dkv_in.astype(jnp.float32), axis=0)
    key_grad = (dkv_sum[:ROWS] * SCALE).astype(jnp.bfloat16)
    value_grad = dkv_sum[ROWS:].astype(jnp.bfloat16)
    return query_grad, key_grad, value_grad


def solution(mesh):
    fine = Mesh(mesh.devices.reshape(SIZES), AXES)
    rows, vec = P(AXES, None), P(AXES)
    return jax.shard_map(
        on_device,
        mesh=fine,
        in_specs=(rows, rows, rows, rows, rows, vec, P(), P()),
        out_specs=(rows, rows, rows),
        check_vma=False,
    )
```

time: 530 us -> 102 us (0.19)
  the two profiles are of different devices: /device:TPU:32 before, /device:TPU:8 now
where the time goes in v1:
time: 102 us; the launch traced here: 101 us
  waiting for transfers between devices  51.3 us (50%)
  starting transfers between devices  20.9 us (20%)
  blocking collectives  17.4 us (17%)
  Pallas kernels  5.38 us (5%)
  local copies, waits for them, and re-layouts  3.57 us (4%)
  other arithmetic  1.58 us (2%)
    all_to_all x1, waiting for transfers between devices, on_device(): lax.all_to_all(jnp.broadcast_to(qg[None], (8, PACK, WIDTH)), 'z', 0, 0, t...  18.2 us
    all_to_all x1, blocking collectives, on_device(): dq_all = lax.all_to_all(dq_pair, 'z', 0, 0, tiled=True)  17.4 us
    all_to_all x1, waiting for transfers between devices, on_device(): lax.all_to_all(jnp.broadcast_to(kv[None], (16, 2 * ROWS, WIDTH)), plane,...  16.6 us
    all_to_all x1, waiting for transfers between devices, on_device(): dkv_in = lax.all_to_all(dkv, plane, 0, 0, tiled=True)  15 us
    all_to_all x1, starting transfers between devices, on_device(): lax.all_to_all(jnp.broadcast_to(qg[None], (8, PACK, WIDTH)), 'z', 0, 0, t...  8.47 us
    all_to_all x1, starting transfers between devices, on_device(): lax.all_to_all(jnp.broadcast_to(kv[None], (16, 2 * ROWS, WIDTH)), plane,...  7.52 us
    all_to_all x1, starting transfers between devices, on_device(): dkv_in = lax.all_to_all(dkv, plane, 0, 0, tiled=True)  4.89 us
    pallas_call x1, Pallas kernels, grads(): pl.pallas_call(grad_kernel, out_shape=(jax.ShapeDtypeStruct((8, ROWS, WID...  3.83 us
  transfers between devices with their start and end apart: 5, of which 4 were waited for; matrix products, arithmetic and copies ran while one was open for 1% of the time, Pallas kernels for 0%

profile of v1, /device:TPU:8, one launch (start us, length us, event | category | flops | bytes accessed | tf_op | source)
XLA Modules:
  0.0 100.8 jit_solution(11975245519311855647)
XLA Ops:
  0.6 0.0 copy-start.2
  0.6 0.0 copy-start.3
  0.7 1.5 %shard_map.103 = bf16[272,128]{1,0:T(8,128)(2,1)} custom-call(bf16[128,128]{1,0:T(8,128)(2,1)} %q_ref.1, bf16[128,128]{1,0:T(8,128)(2,1)} %g_ref.1, bf16[128,128]{1,0:T(8,128)(2,1)} %o_ref.1, f32[1,128]{1,0:T(1,128)} %bitcast.5), custom_call_target="tpu_custom_call" | custom-call | tf_op jit(solution)/shard_map/pallas_call | solution.py:46
  2.2 1.8 %broadcast_in_dim.4 = bf16[8,272,128]{2,1,0:T(8,128)(2,1)} broadcast(bf16[272,128]{1,0:T(8,128)(2,1)} %shard_map.103), dimensions={1,2} | broadcast | bytes 626688 | tf_op jit(solution)/shard_map/broadcast_in_dim | solution.py:180
  4.0 8.5 %all-to-all-start = ((bf16[8,272,128]{2,1,0:T(8,128)(2,1)}), bf16[8,272,128]{2,1,0:T(8,128)(2,1)S(1)}, u32[]{:S(2)}, u32[]{:S(2)}) async-start(bf16[8,272,128]{2,1,0:T(8,128)(2,1)} %broadcast_in_dim.4), calls=%async_computation | async-start | bytes 1114112 | tf_op jit(solution)/shard_map/all_to_all | solution.py:180
  12.4 0.0 copy-done.2
  12.4 0.0 copy-done.3
  12.5 18.2 %all-to-all-done.own_ref = bf16[8,272,128]{2,1,0:T(8,128)(2,1)S(1)} async-done(((bf16[8,272,128]{2,1,0:T(8,128)(2,1)}), bf16[8,272,128]{2,1,0:T(8,128)(2,1)S(1)}, u32[]{:S(2)}, u32[]{:S(2)}) %all-to-all-start) | async-done | bytes 557088 | tf_op jit(solution)/shard_map/all_to_all | solution.py:180
  30.6 1.2 %broadcast_in_dim.5 = bf16[16,256,128]{2,1,0:T(8,128)(2,1)} broadcast(bf16[256,128]{1,0:T(8,128)(2,1)S(1)} %pad_maximum_fusion), dimensions={1,2} | broadcast | bytes 1114112 | tf_op jit(solution)/shard_map/broadcast_in_dim | solution.py:177
  31.8 0.0 copy-start
  31.8 0.0 copy-start.1
  31.8 7.5 %all-to-all-start.1 = ((bf16[16,256,128]{2,1,0:T(8,128)(2,1)}), bf16[16,256,128]{2,1,0:T(8,128)(2,1)S(1)}, u32[]{:S(2)}, u32[]{:S(2)}) async-start(bf16[16,256,128]{2,1,0:T(8,128)(2,1)} %broadcast_in_dim.5), calls=%async_computation.1 | async-start | bytes 2097152 | tf_op jit(solution)/shard_map/all_to_all | solution.py:176
  39.3 0.0 collective-permute-start
  39.3 0.1 pad_add_fusion.where_ref
  39.4 16.6 %all-to-all-done.1.kv_ref = bf16[16,256,128]{2,1,0:T(8,128)(2,1)S(1)} async-done(((bf16[16,256,128]{2,1,0:T(8,128)(2,1)}), bf16[16,256,128]{2,1,0:T(8,128)(2,1)S(1)}, u32[]{:S(2)}, u32[]{:S(2)}) %all-to-all-start.1) | async-done | bytes 1048608 | tf_op jit(solution)/shard_map/all_to_all | solution.py:176
  56.0 0.0 collective-permute-done.other_ref
  56.0 0.0 copy-done
  56.0 0.0 copy-done.1
  56.0 3.8 %shard_map.104 = (bf16[8,128,128]{2,1,0:T(8,128)(2,1)S(1)}, bf16[8,128,128]{2,1,0:T(8,128)(2,1)S(1)}, bf16[16,256,128]{2,1,0:T(8,128)(2,1)}) custom-call(s32[4]{0:T(128)S(1)} %pad_add_fusion.where_ref, s32[16]{0:T(128)S(1)} %copy-done.1, s32[16,16]{1,0:T(8,128)S(1)} %copy-done, bf16[8,272,128]{2,1,0:T(8,128)(2,1)S(1)} %all-to-all-done.own_ref, ...), custom_call_target="tpu_custom_call" | custom-call | tf_op jit(solution)/shard_map/pallas_call | solution.py:147
  59.9 0.0 collective-permute-start.1
  59.9 1.5 %collective-permute-done.1 = bf16[8,128,128]{2,1,0:T(8,128)(2,1)S(1)} collective-permute-done((bf16[8,128,128]{2,1,0:T(8,128)(2,1)S(1)}, bf16[8,128,128]{2,1,0:T(8,128)(2,1)S(1)}, u32[]{:S(2)}, u32[]{:S(2)}) %collective-permute-start.1) | collective-permute-done | bytes 262176 | tf_op jit(solution)/shard_map/ppermute | solution.py:183
  61.4 0.1 add_convert_fusion
  61.5 17.4 %all_to_all.20 = bf16[8,128,128]{2,1,0:T(8,128)(2,1)S(1)} all-to-all(bf16[8,128,128]{2,1,0:T(8,128)(2,1)S(1)} %add_convert_fusion), channel_id=1, replica_groups=mesh['z'=8,'yh'=2,'c'=2,'x'=4,'yl'=2] {'z'}, dimensions={0} | all-to-all | bytes 524288 | tf_op jit(solution)/shard_map/all_to_all | solution.py:186
  78.9 4.9 %all-to-all-start.3 = ((bf16[16,256,128]{2,1,0:T(8,128)(2,1)}), bf16[16,256,128]{2,1,0:T(8,128)(2,1)S(1)}, u32[]{:S(2)}, u32[]{:S(2)}) async-start(bf16[16,256,128]{2,1,0:T(8,128)(2,1)} %get-tuple-element.8), calls=%async_computation.3 | async-start | bytes 2097152 | tf_op jit(solution)/shard_map/all_to_all | solution.py:184
  83.8 0.6 multiply_convert_fusion
  84.4 15.0 %all-to-all-done.3 = bf16[16,256,128]{2,1,0:T(8,128)(2,1)S(1)} async-done(((bf16[16,256,128]{2,1,0:T(8,128)(2,1)}), bf16[16,256,128]{2,1,0:T(8,128)(2,1)S(1)}, u32[]{:S(2)}, u32[]{:S(2)}) %all-to-all-start.3) | async-done | bytes 1048608 | tf_op jit(solution)/shard_map/all_to_all | solution.py:184
  99.4 0.1 convert_reduce_fusion
  99.6 0.6 slice.15
  100.2 0.6 fusion
  (2 shorter events, 0.0 us)
Async XLA Ops:
  0.6 11.8 %copy-start.2 = (bf16[128,128]{1,0:T(8,128)(2,1)S(1)}, bf16[128,128]{1,0:T(8,128)(2,1)}, u32[]{:S(2)}) copy-start(bf16[128,128]{1,0:T(8,128)(2,1)} %param.10) | copy-start | bytes 98308
  0.6 11.8 %copy-start.3 = (bf16[128,128]{1,0:T(8,128)(2,1)S(1)}, bf16[128,128]{1,0:T(8,128)(2,1)}, u32[]{:S(2)}) copy-start(bf16[128,128]{1,0:T(8,128)(2,1)} %param.9) | copy-start | bytes 98308
  4.0 26.7 %all-to-all-start = ((bf16[8,272,128]{2,1,0:T(8,128)(2,1)}), bf16[8,272,128]{2,1,0:T(8,128)(2,1)S(1)}, u32[]{:S(2)}, u32[]{:S(2)}) async-start(bf16[8,272,128]{2,1,0:T(8,128)(2,1)} %broadcast_in_dim.4), calls=%async_computation | async-start | bytes 1114112 | tf_op jit(solution)/shard_map/all_to_all | solution.py:180
  31.8 24.2 %copy-start = (s32[16,16]{1,0:T(8,128)S(1)}, s32[16,16]{1,0:T(8,128)}, u32[]{:S(2)}) copy-start(s32[16,16]{1,0:T(8,128)} %allow_ref.1) | copy-start | bytes 3076
  31.8 24.2 %copy-start.1 = (s32[16]{0:T(128)S(1)}, s32[16]{0:T(128)}, u32[]{:S(2)}) copy-start(s32[16]{0:T(128)} %len_ref.1) | copy-start | bytes 196
  31.8 24.2 %all-to-all-start.1 = ((bf16[16,256,128]{2,1,0:T(8,128)(2,1)}), bf16[16,256,128]{2,1,0:T(8,128)(2,1)S(1)}, u32[]{:S(2)}, u32[]{:S(2)}) async-start(bf16[16,256,128]{2,1,0:T(8,128)(2,1)} %broadcast_in_dim.5), calls=%async_computation.1 | async-start | bytes 2097152 | tf_op jit(solution)/shard_map/all_to_all | solution.py:176
  39.3 16.7 %collective-permute-start = (bf16[8,272,128]{2,1,0:T(8,128)(2,1)S(1)}, bf16[8,272,128]{2,1,0:T(8,128)(2,1)S(1)}, u32[]{:S(2)}, u32[]{:S(2)}) collective-permute-start(bf16[8,272,128]{2,1,0:T(8,128)(2,1)S(1)} %all-to-all-done.own_ref), channel_id=1, source_target_pairs={{0,8},{8,0},{1,9},{9,1},{2,10},{10,2},{3,11},{11,3},{4,12},{12,4},... | collective-permute-start | bytes 1671176 | tf_op jit(solution)/shard_map/ppermute | solution.py:181
  59.9 1.5 %collective-permute-start.1 = (bf16[8,128,128]{2,1,0:T(8,128)(2,1)S(1)}, bf16[8,128,128]{2,1,0:T(8,128)(2,1)S(1)}, u32[]{:S(2)}, u32[]{:S(2)}) collective-permute-start(bf16[8,128,128]{2,1,0:T(8,128)(2,1)S(1)} %get-tuple-element.7), channel_id=1, source_target_pairs={{0,8},{8,0},{1,9},{9,1},{2,10},{10,2},{3,11},{11,3},{4,12},{12,4},... | collective-permute-start | bytes 786440 | tf_op jit(solution)/shard_map/ppermute | solution.py:183
  78.9 20.5 %all-to-all-start.3 = ((bf16[16,256,128]{2,1,0:T(8,128)(2,1)}), bf16[16,256,128]{2,1,0:T(8,128)(2,1)S(1)}, u32[]{:S(2)}, u32[]{:S(2)}) async-start(bf16[16,256,128]{2,1,0:T(8,128)(2,1)} %get-tuple-element.8), calls=%async_computation.3 | async-start | bytes 2097152 | tf_op jit(solution)/shard_map/all_to_all | solution.py:184

commit v2 on v1

v2 whole, which is shorter than its diff:
```python
import math

import jax
import jax.numpy as jnp
import numpy as np
from jax import lax
from jax.experimental import pallas as pl
from jax.experimental.pallas import tpu as pltpu
from jax.sharding import Mesh, PartitionSpec as P

AXES = ("z", "yh", "c", "x", "yl")
SIZES = (8, 2, 2, 4, 2)
PLANE = ("yh", "x", "yl")
ROWS = 128
WIDTH = 128
NDOCS = 16
TILE = 2048
RUN = 1024
CHUNK = 256
PACK = 272
FAR = 1 << 30
LOG2E = math.log2(math.e)
SCALE = 128.0 ** -0.5


def pairs_along_z(k, both_ways, back):
    pairs = []
    for i in range(256):
        z, yh, c, x, yl = (int(v) for v in np.unravel_index(i, SIZES))
        t = z - k + 8 if both_ways and c == 1 else z + k
        if z < t < 8:
            j = int(np.ravel_multi_index((t, yh, c, x, yl), SIZES))
            pairs.append((j, i) if back else (i, j))
    return pairs


def split3(x):
    a = x.astype(jnp.bfloat16)
    r = x - a.astype(jnp.float32)
    b = r.astype(jnp.bfloat16)
    c = (r - b.astype(jnp.float32)).astype(jnp.bfloat16)
    return a, b, c


def pack_kernel(q_ref, g_ref, o_ref, lse_ref, out_ref):
    prod = g_ref[...].astype(jnp.float32) * o_ref[...].astype(jnp.float32)
    delta = jnp.sum(prod.T, axis=0, keepdims=True)
    lse2 = lse_ref[...] * LOG2E
    parts = split3(lse2) + split3(delta)
    stats = jnp.concatenate(
        [p.astype(jnp.float32) for p in parts] + [jnp.zeros((10, ROWS), jnp.float32)], axis=0
    ).astype(jnp.bfloat16)
    for n in range(16):
        out_ref[n, 0:128] = q_ref[...]
        out_ref[n, 128:256] = g_ref[...]
        out_ref[n, 256:272] = stats


def pack(q, g, o, lse):
    return pl.pallas_call(
        pack_kernel,
        out_shape=jax.ShapeDtypeStruct((16, PACK, WIDTH), jnp.bfloat16),
    )(q, g, o, lse)


def grad_kernel(
    where_ref, len_ref, allow_ref, own_ref, other_ref, kv0_ref, kv4_ref, kv1_ref, kv2_ref, kv3_ref,
    dqo_ref, dqx_ref, d0_ref, d4_ref, d1_ref, d2_ref, d3_ref,
    k_s, v_s, kt_s, dk_acc, dv_acc, dqt_acc, stat_s, start_s, base_s,
):
    z, yh, c, koff = where_ref[0], where_ref[1], where_ref[2], where_ref[3]
    ends = []
    total = jnp.int32(0)
    for d in range(NDOCS):
        total = total + len_ref[d]
        ends.append(total)

    wide = ((kv1_ref, 1), (kv2_ref, 2), (kv3_ref, 3))
    for half, ref in enumerate((kv0_ref, kv4_ref)):
        k_s[0, half * ROWS : (half + 1) * ROWS] = ref[0:128]
        v_s[0, half * ROWS : (half + 1) * ROWS] = ref[128:256]
    for ref, s in wide:
        for half in range(2):
            k_s[s, half * ROWS : (half + 1) * ROWS] = ref[half, 0:128]
            v_s[s, half * ROWS : (half + 1) * ROWS] = ref[half, 128:256]
    for s in range(4):
        kt_s[s] = k_s[s].T
    dk_acc[...] = jnp.zeros_like(dk_acc)
    dv_acc[...] = jnp.zeros_like(dv_acc)
    dqt_acc[...] = jnp.zeros_like(dqt_acc)

    in_plane = yh * TILE + koff
    base_s[0] = z
    base_s[1] = z - 4
    for s in range(1, 4):
        zk = jnp.where(c == 0, z - s, z + s - 8)
        base_s[2 * s] = zk
        base_s[2 * s + 1] = zk

    lane = lax.broadcasted_iota(jnp.int32, (1, RUN), 1)
    for h, ref in enumerate((own_ref, other_ref)):
        cq = c if h == 0 else 1 - c
        for t in range(2):
            st = jnp.concatenate(
                [ref[8 * t + n, 256:272].astype(jnp.float32) for n in range(8)], axis=1
            )
            stat_s[2 * h + t, 0:1] = st[0:1] + st[1:2] + st[2:3]
            stat_s[2 * h + t, 1:2] = st[3:4] + st[4:5] + st[5:6]
            pos = z * (2 * TILE) + t * TILE + cq * RUN + lane
            start = jnp.zeros_like(pos)
            for e in ends:
                start = jnp.where(pos >= e, e, start)
            start_s[2 * h + t, 0:1] = start

    def first_start(pos):
        s = jnp.int32(0)
        for e in ends:
            s = jnp.where(e <= pos, e, s)
        return s

    row = lax.broadcasted_iota(jnp.int32, (ROWS, 1), 0)

    def slot_step(s, carry):
        for h, ref in enumerate((own_ref, other_ref)):
            cq = c if h == 0 else 1 - c

            def run_step(t, carry2):
                p0 = z * (2 * TILE) + t * TILE + cq * RUN
                s0 = first_start(p0)
                bases = []
                for half in range(2):
                    zk = base_s[2 * s + half]
                    ck = jnp.where((half == 0) | (s == 0), c, 1 - c)
                    b = zk * (2 * TILE) + ck * RUN + in_plane
                    ok = allow_ref[2 * z + t, jnp.maximum(2 * zk + yh, 0)] == 1
                    live = ok & (zk >= 0) & (b <= p0 + RUN - 1) & (b + ROWS - 1 >= s0)
                    bases.append((live, b))

                @pl.when(bases[0][0] | bases[1][0])
                def _unit():
                    k = k_s[s]
                    v = v_s[s]
                    kt = kt_s[s]
                    key = jnp.concatenate(
                        [jnp.where(live, b, FAR) + row for live, b in bases], axis=0
                    )
                    dk = jnp.zeros((CHUNK, WIDTH), jnp.float32)
                    dv = jnp.zeros((CHUNK, WIDTH), jnp.float32)
                    for n in range(RUN // CHUNK):
                        cols = slice(n * CHUNK, (n + 1) * CHUNK)
                        q = ref[pl.ds(8 * t + 2 * n, 2), 0:128, :].reshape(CHUNK, WIDTH)
                        g = ref[pl.ds(8 * t + 2 * n, 2), 128:256, :].reshape(CHUNK, WIDTH)
                        lse2 = stat_s[2 * h + t, 0:1, cols]
                        delta = stat_s[2 * h + t, 1:2, cols]
                        start = start_s[2 * h + t, 0:1, cols]
                        pos = p0 + lane[:, cols]
                        sc = lax.dot_general(
                            k, q, (((1,), (1,)), ((), ())), preferred_element_type=jnp.float32
                        )
                        dp = lax.dot_general(
                            v, g, (((1,), (1,)), ((), ())), preferred_element_type=jnp.float32
                        )
                        vis = (key >= start) & (key <= pos)
                        p = jnp.where(vis, jnp.exp2(sc * (SCALE * LOG2E) - lse2), 0.0)
                        pb = p.astype(jnp.bfloat16)
                        ds = (p * (dp - delta)).astype(jnp.bfloat16)
                        dv = dv + jnp.dot(pb, g, preferred_element_type=jnp.float32)
                        dk = dk + jnp.dot(ds, q, preferred_element_type=jnp.float32)
                        dqt_acc[2 * h + t, :, cols] += jnp.dot(
                            kt, ds, preferred_element_type=jnp.float32
                        )
                    dk_acc[s] += dk
                    dv_acc[s] += dv

                return carry2

            lax.fori_loop(0, 2, run_step, 0)
        return carry

    lax.fori_loop(0, 4, slot_step, 0)

    for h, out in enumerate((dqo_ref, dqx_ref)):
        for t in range(2):
            out[8 * t : 8 * t + 8] = (
                dqt_acc[2 * h + t].T.astype(jnp.bfloat16).reshape(8, ROWS, WIDTH)
            )
    for half, out in enumerate((d0_ref, d4_ref)):
        out[0:128] = dk_acc[0, half * ROWS : (half + 1) * ROWS].astype(jnp.bfloat16)
        out[128:256] = dv_acc[0, half * ROWS : (half + 1) * ROWS].astype(jnp.bfloat16)
    for out, s in ((d1_ref, 1), (d2_ref, 2), (d3_ref, 3)):
        for half in range(2):
            out[half, 0:128] = dk_acc[s, half * ROWS : (half + 1) * ROWS].astype(jnp.bfloat16)
            out[half, 128:256] = dv_acc[s, half * ROWS : (half + 1) * ROWS].astype(jnp.bfloat16)


def grads(where, doc_lengths, tile_allowed, own, other, kv0, kv4, kv1, kv2, kv3):
    smem = pl.BlockSpec(memory_space=pltpu.SMEM)
    vmem = pl.BlockSpec(memory_space=pltpu.VMEM)
    bf, f32 = jnp.bfloat16, jnp.float32
    one = jax.ShapeDtypeStruct((2 * ROWS, WIDTH), bf)
    two = jax.ShapeDtypeStruct((2, 2 * ROWS, WIDTH), bf)
    dq = jax.ShapeDtypeStruct((16, ROWS, WIDTH), bf)
    return pl.pallas_call(
        grad_kernel,
        out_shape=(dq, dq, one, one, two, two, two),
        in_specs=[smem, smem, smem] + [vmem] * 7,
        out_specs=(vmem,) * 7,
        scratch_shapes=[
            pltpu.VMEM((4, CHUNK, WIDTH), bf),
            pltpu.VMEM((4, CHUNK, WIDTH), bf),
            pltpu.VMEM((4, WIDTH, CHUNK), bf),
            pltpu.VMEM((4, CHUNK, WIDTH), f32),
            pltpu.VMEM((4, CHUNK, WIDTH), f32),
            pltpu.VMEM((4, WIDTH, RUN), f32),
            pltpu.VMEM((4, 8, RUN), f32),
            pltpu.VMEM((4, 8, RUN), jnp.int32),
            pltpu.SMEM((8,), jnp.int32),
        ],
        compiler_params=pltpu.CompilerParams(vmem_limit_bytes=32 * 1024 * 1024),
    )(where, doc_lengths, tile_allowed, own, other, kv0, kv4, kv1, kv2, kv3)


def on_device(
    queries, key_rows, value_rows, outputs, out_grad, log_sums, doc_lengths, tile_allowed
):
    z, yh, c = lax.axis_index("z"), lax.axis_index("yh"), lax.axis_index("c")
    koff = (lax.axis_index("x") * 2 + lax.axis_index("yl")) * ROWS
    where = jnp.stack([z, yh, c, koff]).astype(jnp.int32)
    swap = [(0, 1), (1, 0)]

    def along_z(x, k, both_ways=True, back=False):
        return lax.ppermute(x, AXES, pairs_along_z(k, both_ways, back))

    packed = pack(queries, out_grad, outputs, log_sums.reshape(1, ROWS))
    own = lax.all_to_all(packed, PLANE, 0, 0, tiled=True)

    kv0 = jnp.concatenate([key_rows, value_rows], axis=0)
    kv_pair = jnp.stack([kv0, lax.ppermute(kv0, "c", swap)])
    kv1, kv2, kv3 = (along_z(kv_pair, k) for k in (1, 2, 3))
    kv4 = along_z(kv0, 4, both_ways=False)
    other = lax.ppermute(own, "c", swap)

    dq_own, dq_other, d0, d4, d1, d2, d3 = grads(
        where, doc_lengths, tile_allowed, own, other, kv0, kv4, kv1, kv2, kv3
    )
    f32 = jnp.float32
    dq_in = lax.ppermute(dq_other, "c", swap)
    e1, e2, e3 = (along_z(d, k, back=True) for k, d in ((1, d1), (2, d2), (3, d3)))
    e4 = along_z(d4, 4, both_ways=False, back=True)
    dq_pair = (dq_own.astype(f32) + dq_in.astype(f32)).astype(jnp.bfloat16)
    dq_all = lax.all_to_all(dq_pair, PLANE, 0, 0, tiled=True)
    back = e1.astype(f32) + e2.astype(f32) + e3.astype(f32)
    from_core = lax.ppermute(back[1].astype(jnp.bfloat16), "c", swap)
    dkv = back[0] + e4.astype(f32) + d0.astype(f32) + from_core.astype(f32)
    query_grad = (jnp.sum(dq_all.astype(f32), axis=0) * SCALE).astype(jnp.bfloat16)
    key_grad = (dkv[:ROWS] * SCALE).astype(jnp.bfloat16)
    value_grad = dkv[ROWS:].astype(jnp.bfloat16)
    return query_grad, key_grad, value_grad


def solution(mesh):
    fine = Mesh(mesh.devices.reshape(SIZES), AXES)
    rows, vec = P(AXES, None), P(AXES)
    return jax.shard_map(
        on_device,
        mesh=fine,
        in_specs=(rows, rows, rows, rows, rows, vec, P(), P()),
        out_specs=(rows, rows, rows),
        check_vma=False,
    )
```

time: 102 us -> 99.9 us (0.979)
  the two profiles are of different devices: /device:TPU:8 before, /device:TPU:64 now
where the time goes in v2:
time: 99.9 us; the launch traced here: 99.7 us
  waiting for transfers between devices  36.8 us (37%)
  starting transfers between devices  27.7 us (28%)
  blocking collectives  25 us (25%)
  Pallas kernels  6.37 us (6%)
  other arithmetic  2.43 us (2%)
    all_to_all x1, blocking collectives, on_device(): own = lax.all_to_all(packed, PLANE, 0, 0, tiled=True)  25 us
    ppermute x8, waiting for transfers between devices, along_z(): return lax.ppermute(x, AXES, pairs_along_z(k, both_ways, back))  23.6 us
    ppermute x8, starting transfers between devices, along_z(): return lax.ppermute(x, AXES, pairs_along_z(k, both_ways, back))  22.1 us
    all_to_all x1, waiting for transfers between devices, on_device(): dq_all = lax.all_to_all(dq_pair, PLANE, 0, 0, tiled=True)  11 us
    all_to_all x1, starting transfers between devices, on_device(): dq_all = lax.all_to_all(dq_pair, PLANE, 0, 0, tiled=True)  4.77 us
    pallas_call x1, Pallas kernels, grads(): pl.pallas_call(grad_kernel, out_shape=(dq, dq, one, one, two, two, two),...  4.43 us
    ppermute x1, waiting for transfers between devices, on_device(): kv_pair = jnp.stack([kv0, lax.ppermute(kv0, 'c', swap)])  2.22 us
  transfers between devices with their start and end apart: 13, of which 6 were waited for; matrix products, arithmetic and copies ran while one was open for 2% of the time, Pallas kernels for 0%

profile of v2, /device:TPU:64, one launch (start us, length us, event | category | flops | bytes accessed | tf_op | source)
XLA Modules:
  0.0 99.7 jit_solution(8999039142379621671)
XLA Ops:
  0.6 1.9 %shard_map.103 = bf16[16,272,128]{2,1,0:T(8,128)(2,1)} custom-call(bf16[128,128]{1,0:T(8,128)(2,1)} %q_ref.1, bf16[128,128]{1,0:T(8,128)(2,1)} %g_ref.1, bf16[128,128]{1,0:T(8,128)(2,1)} %o_ref.1, f32[1,128]{1,0:T(1,128)} %bitcast.19), custom_call_target="tpu_custom_call" | custom-call | tf_op jit(solution)/shard_map/pallas_call | solution.py:60
  2.6 0.0 copy-start.2
  2.6 0.0 copy-start.3
  2.6 0.0 copy-start
  2.6 0.0 copy-start.1
  2.6 25.0 %all_to_all.10.own_ref = bf16[16,272,128]{2,1,0:T(8,128)(2,1)S(1)} all-to-all(bf16[16,272,128]{2,1,0:T(8,128)(2,1)} %shard_map.103), channel_id=1, replica_groups=mesh['z'=8,'yh'=2,'c'=2,'x'=4,'yl'=2] {'yh','x','yl'}, dimensions={0} | all-to-all | bytes 2228224 | tf_op jit(solution)/shard_map/all_to_all | solution.py:235
  27.6 0.0 collective-permute-start
  27.6 0.0 copy-done.2
  27.6 0.0 copy-done.3
  27.6 0.6 collective-permute-start.2
  28.2 2.2 %collective-permute-done.2 = bf16[256,128]{1,0:T(8,128)(2,1)S(1)} collective-permute-done((bf16[256,128]{1,0:T(8,128)(2,1)S(1)}, bf16[256,128]{1,0:T(8,128)(2,1)S(1)}, u32[]{:S(2)}, u32[]{:S(2)}) %collective-permute-start.2) | collective-permute-done | bytes 65568 | tf_op jit(solution)/shard_map/ppermute | solution.py:238
  30.4 6.8 %collective-permute-start.5 = (bf16[2,256,128]{2,1,0:T(8,128)(2,1)S(1)}, bf16[2,256,128]{2,1,0:T(8,128)(2,1)S(1)}, u32[]{:S(2)}, u32[]{:S(2)}) collective-permute-start(bf16[2,256,128]{2,1,0:T(8,128)(2,1)S(1)} %pad_maximum_fusion), channel_id=1, source_target_pairs={{0,96},{1,97},{2,98},{3,99},{4,100},{5,101},{6,102},{7,103},{8,168... | collective-permute-start | bytes 393224 | tf_op jit(solution)/shard_map/ppermute | solution.py:232
  37.3 3.4 %collective-permute-start.4 = (bf16[2,256,128]{2,1,0:T(8,128)(2,1)S(1)}, bf16[2,256,128]{2,1,0:T(8,128)(2,1)S(1)}, u32[]{:S(2)}, u32[]{:S(2)}) collective-permute-start(bf16[2,256,128]{2,1,0:T(8,128)(2,1)S(1)} %pad_maximum_fusion), channel_id=1, source_target_pairs={{0,64},{1,65},{2,66},{3,67},{4,68},{5,69},{6,70},{7,71},{8,200},{9... | collective-permute-start | bytes 393224 | tf_op jit(solution)/shard_map/ppermute | solution.py:232
  40.7 1.9 %collective-permute-start.3 = (bf16[2,256,128]{2,1,0:T(8,128)(2,1)S(1)}, bf16[2,256,128]{2,1,0:T(8,128)(2,1)S(1)}, u32[]{:S(2)}, u32[]{:S(2)}) collective-permute-start(bf16[2,256,128]{2,1,0:T(8,128)(2,1)S(1)} %pad_maximum_fusion), channel_id=1, source_target_pairs={{0,32},{1,33},{2,34},{3,35},{4,36},{5,37},{6,38},{7,39},{8,232},{9... | collective-permute-start | bytes 393224 | tf_op jit(solution)/shard_map/ppermute | solution.py:232
  42.6 1.3 %collective-permute-start.1 = (bf16[256,128]{1,0:T(8,128)(2,1)S(1)}, bf16[256,128]{1,0:T(8,128)(2,1)S(1)}, u32[]{:S(2)}, u32[]{:S(2)}) collective-permute-start(bf16[256,128]{1,0:T(8,128)(2,1)S(1)} %constant_dynamic-update-slice_fusion.kv0_ref), channel_id=1, source_target_pairs={{0,128},{1,129},{2,130},{3,131},{4,132},{5,133},{6,134},{7,135},{8... | collective-permute-start | bytes 196616 | tf_op jit(solution)/shard_map/ppermute | solution.py:232
  43.9 0.1 pad_add_fusion.where_ref
  44.0 4.5 %collective-permute-done.1.kv4_ref = bf16[256,128]{1,0:T(8,128)(2,1)S(1)} collective-permute-done((bf16[256,128]{1,0:T(8,128)(2,1)S(1)}, bf16[256,128]{1,0:T(8,128)(2,1)S(1)}, u32[]{:S(2)}, u32[]{:S(2)}) %collective-permute-start.1) | collective-permute-done | bytes 65568 | tf_op jit(solution)/shard_map/ppermute | solution.py:232
  48.5 0.0 collective-permute-done.5.kv3_ref
  48.5 0.0 collective-permute-done.4.kv2_ref
  48.5 0.0 collective-permute-done.3.kv1_ref
  48.5 0.0 collective-permute-done.other_ref
  48.5 0.0 copy-done
  48.5 0.0 copy-done.1
  48.5 4.4 %shard_map.104 = (bf16[16,128,128]{2,1,0:T(8,128)(2,1)S(1)}, bf16[16,128,128]{2,1,0:T(8,128)(2,1)S(1)}, bf16[256,128]{1,0:T(8,128)(2,1)S(1)}, bf16[256,128]{1,0:...) custom-call(s32[4]{0:T(128)S(1)} %pad_add_fusion.where_ref, ...), custom_call_target="tpu_custom_call" | custom-call | tf_op jit(solution)/shard_map/pallas_call | solution.py:203
  53.0 4.2 %collective-permute-start.7 = (bf16[2,256,128]{2,1,0:T(8,128)(2,1)S(1)}, bf16[2,256,128]{2,1,0:T(8,128)(2,1)S(1)}, u32[]{:S(2)}, u32[]{:S(2)}) collective-permute-start(bf16[2,256,128]{2,1,0:T(8,128)(2,1)S(1)} %get-tuple-element.12), channel_id=1, source_target_pairs={{32,0},{33,1},{34,2},{35,3},{36,4},{37,5},{38,6},{39,7},{232,8},{2... | collective-permute-start | bytes 393224 | tf_op jit(solution)/shard_map/ppermute | solution.py:232
  57.2 1.9 %collective-permute-start.8 = (bf16[2,256,128]{2,1,0:T(8,128)(2,1)S(1)}, bf16[2,256,128]{2,1,0:T(8,128)(2,1)S(1)}, u32[]{:S(2)}, u32[]{:S(2)}) collective-permute-start(bf16[2,256,128]{2,1,0:T(8,128)(2,1)S(1)} %get-tuple-element.13), channel_id=1, source_target_pairs={{64,0},{65,1},{66,2},{67,3},{68,4},{69,5},{70,6},{71,7},{200,8},{2... | collective-permute-start | bytes 393224 | tf_op jit(solution)/shard_map/ppermute | solution.py:232
  59.1 1.3 %collective-permute-start.9 = (bf16[2,256,128]{2,1,0:T(8,128)(2,1)S(1)}, bf16[2,256,128]{2,1,0:T(8,128)(2,1)S(1)}, u32[]{:S(2)}, u32[]{:S(2)}) collective-permute-start(bf16[2,256,128]{2,1,0:T(8,128)(2,1)S(1)} %get-tuple-element.14), channel_id=1, source_target_pairs={{96,0},{97,1},{98,2},{99,3},{100,4},{101,5},{102,6},{103,7},{168,8... | collective-permute-start | bytes 393224 | tf_op jit(solution)/shard_map/ppermute | solution.py:232
  60.4 0.1 collective-permute-start.6
  60.5 1.3 %collective-permute-start.10 = (bf16[256,128]{1,0:T(8,128)(2,1)S(1)}, bf16[256,128]{1,0:T(8,128)(2,1)S(1)}, u32[]{:S(2)}, u32[]{:S(2)}) collective-permute-start(bf16[256,128]{1,0:T(8,128)(2,1)S(1)} %get-tuple-element.15), channel_id=1, source_target_pairs={{128,0},{129,1},{130,2},{131,3},{132,4},{133,5},{134,6},{135,7},{1... | collective-permute-start | bytes 196616 | tf_op jit(solution)/shard_map/ppermute | solution.py:232
  61.8 4.9 %collective-permute-done.7 = bf16[2,256,128]{2,1,0:T(8,128)(2,1)S(1)} collective-permute-done((bf16[2,256,128]{2,1,0:T(8,128)(2,1)S(1)}, bf16[2,256,128]{2,1,0:T(8,128)(2,1)S(1)}, u32[]{:S(2)}, u32[]{:S(2)}) %collective-permute-start.7) | collective-permute-done | bytes 131104 | tf_op jit(solution)/shard_map/ppermute | solution.py:232
  66.7 5.1 %collective-permute-done.8 = bf16[2,256,128]{2,1,0:T(8,128)(2,1)S(1)} collective-permute-done((bf16[2,256,128]{2,1,0:T(8,128)(2,1)S(1)}, bf16[2,256,128]{2,1,0:T(8,128)(2,1)S(1)}, u32[]{:S(2)}, u32[]{:S(2)}) %collective-permute-start.8) | collective-permute-done | bytes 131104 | tf_op jit(solution)/shard_map/ppermute | solution.py:232
  71.8 9.1 %collective-permute-done.9 = bf16[2,256,128]{2,1,0:T(8,128)(2,1)S(1)} collective-permute-done((bf16[2,256,128]{2,1,0:T(8,128)(2,1)S(1)}, bf16[2,256,128]{2,1,0:T(8,128)(2,1)S(1)}, u32[]{:S(2)}, u32[]{:S(2)}) %collective-permute-start.9) | collective-permute-done | bytes 131104 | tf_op jit(solution)/shard_map/ppermute | solution.py:232
  80.9 0.1 collective-permute-start.11
  81.0 0.0 collective-permute-done.6
  81.1 0.9 add_convert_fusion
  82.0 4.8 %all-to-all-start.1 = ((bf16[16,128,128]{2,1,0:T(8,128)(2,1)}), bf16[16,128,128]{2,1,0:T(8,128)(2,1)S(1)}, u32[]{:S(2)}, u32[]{:S(2)}) async-start(bf16[16,128,128]{2,1,0:T(8,128)(2,1)} %add_convert_fusion), calls=%async_computation.1 | async-start | bytes 1048576 | tf_op jit(solution)/shard_map/all_to_all | solution.py:251
  86.8 0.0 collective-permute-done.10
  86.8 0.0 collective-permute-done.11
  86.8 0.6 slice.36
  87.5 0.6 fusion.4
  88.1 11.0 %all-to-all-done.1 = bf16[16,128,128]{2,1,0:T(8,128)(2,1)S(1)} async-done(((bf16[16,128,128]{2,1,0:T(8,128)(2,1)}), bf16[16,128,128]{2,1,0:T(8,128)(2,1)S(1)}, u32[]{:S(2)}, u32[]{:S(2)}) %all-to-all-start.1) | async-done | bytes 524320 | tf_op jit(solution)/shard_map/all_to_all | solution.py:251
  99.0 0.1 convert_reduce_fusion
  99.1 0.6 multiply_convert_fusion
  (6 shorter events, 0.1 us)
Async XLA Ops:
  2.6 25.0 %copy-start.2 = (bf16[128,128]{1,0:T(8,128)(2,1)S(1)}, bf16[128,128]{1,0:T(8,128)(2,1)}, u32[]{:S(2)}) copy-start(bf16[128,128]{1,0:T(8,128)(2,1)} %param.9) | copy-start | bytes 98308
  2.6 25.0 %copy-start.3 = (bf16[128,128]{1,0:T(8,128)(2,1)S(1)}, bf16[128,128]{1,0:T(8,128)(2,1)}, u32[]{:S(2)}) copy-start(bf16[128,128]{1,0:T(8,128)(2,1)} %param.10) | copy-start | bytes 98308
  2.6 45.9 %copy-start = (s32[16,16]{1,0:T(8,128)S(1)}, s32[16,16]{1,0:T(8,128)}, u32[]{:S(2)}) copy-start(s32[16,16]{1,0:T(8,128)} %allow_ref.1) | copy-start | bytes 3076
  2.6 45.9 %copy-start.1 = (s32[16]{0:T(128)S(1)}, s32[16]{0:T(128)}, u32[]{:S(2)}) copy-start(s32[16]{0:T(128)} %len_ref.1) | copy-start | bytes 196
  27.6 20.9 %collective-permute-start = (bf16[16,272,128]{2,1,0:T(8,128)(2,1)S(1)}, bf16[16,272,128]{2,1,0:T(8,128)(2,1)S(1)}, u32[]{:S(2)}, u32[]{:S(2)}) collective-permute-start(bf16[16,272,128]{2,1,0:T(8,128)(2,1)S(1)} %all_to_all.10.own_ref), channel_id=1, source_target_pairs={{0,8},{8,0},{1,9},{9,1},{2,10},{10,2},{3,11},{11,3},{4,12},{12,4},... | collective-permute-start | bytes 3342344 | tf_op jit(solution)/shard_map/ppermute | solution.py:241
  27.6 2.8 %collective-permute-start.2 = (bf16[256,128]{1,0:T(8,128)(2,1)S(1)}, bf16[256,128]{1,0:T(8,128)(2,1)S(1)}, u32[]{:S(2)}, u32[]{:S(2)}) collective-permute-start(bf16[256,128]{1,0:T(8,128)(2,1)S(1)} %constant_dynamic-update-slice_fusion.kv0_ref), channel_id=1, source_target_pairs={{0,8},{8,0},{1,9},{9,1},{2,10},{10,2},{3,11},{11,3},{4,12},{12,4},... | collective-permute-start | bytes 196616 | tf_op jit(solution)/shard_map/ppermute | solution.py:238
  30.4 18.1 %collective-permute-start.5 = (bf16[2,256,128]{2,1,0:T(8,128)(2,1)S(1)}, bf16[2,256,128]{2,1,0:T(8,128)(2,1)S(1)}, u32[]{:S(2)}, u32[]{:S(2)}) collective-permute-start(bf16[2,256,128]{2,1,0:T(8,128)(2,1)S(1)} %pad_maximum_fusion), channel_id=1, source_target_pairs={{0,96},{1,97},{2,98},{3,99},{4,100},{5,101},{6,102},{7,103},{8,168... | collective-permute-start | bytes 393224 | tf_op jit(solution)/shard_map/ppermute | solution.py:232
  37.3 11.2 %collective-permute-start.4 = (bf16[2,256,128]{2,1,0:T(8,128)(2,1)S(1)}, bf16[2,256,128]{2,1,0:T(8,128)(2,1)S(1)}, u32[]{:S(2)}, u32[]{:S(2)}) collective-permute-start(bf16[2,256,128]{2,1,0:T(8,128)(2,1)S(1)} %pad_maximum_fusion), channel_id=1, source_target_pairs={{0,64},{1,65},{2,66},{3,67},{4,68},{5,69},{6,70},{7,71},{8,200},{9... | collective-permute-start | bytes 393224 | tf_op jit(solution)/shard_map/ppermute | solution.py:232
  40.7 7.8 %collective-permute-start.3 = (bf16[2,256,128]{2,1,0:T(8,128)(2,1)S(1)}, bf16[2,256,128]{2,1,0:T(8,128)(2,1)S(1)}, u32[]{:S(2)}, u32[]{:S(2)}) collective-permute-start(bf16[2,256,128]{2,1,0:T(8,128)(2,1)S(1)} %pad_maximum_fusion), channel_id=1, source_target_pairs={{0,32},{1,33},{2,34},{3,35},{4,36},{5,37},{6,38},{7,39},{8,232},{9... | collective-permute-start | bytes 393224 | tf_op jit(solution)/shard_map/ppermute | solution.py:232
  42.6 5.9 %collective-permute-start.1 = (bf16[256,128]{1,0:T(8,128)(2,1)S(1)}, bf16[256,128]{1,0:T(8,128)(2,1)S(1)}, u32[]{:S(2)}, u32[]{:S(2)}) collective-permute-start(bf16[256,128]{1,0:T(8,128)(2,1)S(1)} %constant_dynamic-update-slice_fusion.kv0_ref), channel_id=1, source_target_pairs={{0,128},{1,129},{2,130},{3,131},{4,132},{5,133},{6,134},{7,135},{8... | collective-permute-start | bytes 196616 | tf_op jit(solution)/shard_map/ppermute | solution.py:232
  53.0 13.7 %collective-permute-start.7 = (bf16[2,256,128]{2,1,0:T(8,128)(2,1)S(1)}, bf16[2,256,128]{2,1,0:T(8,128)(2,1)S(1)}, u32[]{:S(2)}, u32[]{:S(2)}) collective-permute-start(bf16[2,256,128]{2,1,0:T(8,128)(2,1)S(1)} %get-tuple-element.12), channel_id=1, source_target_pairs={{32,0},{33,1},{34,2},{35,3},{36,4},{37,5},{38,6},{39,7},{232,8},{2... | collective-permute-start | bytes 393224 | tf_op jit(solution)/shard_map/ppermute | solution.py:232
  57.2 14.6 %collective-permute-start.8 = (bf16[2,256,128]{2,1,0:T(8,128)(2,1)S(1)}, bf16[2,256,128]{2,1,0:T(8,128)(2,1)S(1)}, u32[]{:S(2)}, u32[]{:S(2)}) collective-permute-start(bf16[2,256,128]{2,1,0:T(8,128)(2,1)S(1)} %get-tuple-element.13), channel_id=1, source_target_pairs={{64,0},{65,1},{66,2},{67,3},{68,4},{69,5},{70,6},{71,7},{200,8},{2... | collective-permute-start | bytes 393224 | tf_op jit(solution)/shard_map/ppermute | solution.py:232
  59.1 21.8 %collective-permute-start.9 = (bf16[2,256,128]{2,1,0:T(8,128)(2,1)S(1)}, bf16[2,256,128]{2,1,0:T(8,128)(2,1)S(1)}, u32[]{:S(2)}, u32[]{:S(2)}) collective-permute-start(bf16[2,256,128]{2,1,0:T(8,128)(2,1)S(1)} %get-tuple-element.14), channel_id=1, source_target_pairs={{96,0},{97,1},{98,2},{99,3},{100,4},{101,5},{102,6},{103,7},{168,8... | collective-permute-start | bytes 393224 | tf_op jit(solution)/shard_map/ppermute | solution.py:232
  60.4 20.7 %collective-permute-start.6 = (bf16[16,128,128]{2,1,0:T(8,128)(2,1)S(1)}, bf16[16,128,128]{2,1,0:T(8,128)(2,1)S(1)}, u32[]{:S(2)}, u32[]{:S(2)}) collective-permute-start(bf16[16,128,128]{2,1,0:T(8,128)(2,1)S(1)} %get-tuple-element.11), channel_id=1, source_target_pairs={{0,8},{8,0},{1,9},{9,1},{2,10},{10,2},{3,11},{11,3},{4,12},{12,4},... | collective-permute-start | bytes 1572872 | tf_op jit(solution)/shard_map/ppermute | solution.py:247
  60.5 26.3 %collective-permute-start.10 = (bf16[256,128]{1,0:T(8,128)(2,1)S(1)}, bf16[256,128]{1,0:T(8,128)(2,1)S(1)}, u32[]{:S(2)}, u32[]{:S(2)}) collective-permute-start(bf16[256,128]{1,0:T(8,128)(2,1)S(1)} %get-tuple-element.15), channel_id=1, source_target_pairs={{128,0},{129,1},{130,2},{131,3},{132,4},{133,5},{134,6},{135,7},{1... | collective-permute-start | bytes 196616 | tf_op jit(solution)/shard_map/ppermute | solution.py:232
  80.9 5.8 %collective-permute-start.11 = (bf16[256,128]{1,0:T(8,128)(2,1)S(1)}, bf16[256,128]{1,0:T(8,128)(2,1)S(1)}, u32[]{:S(2)}, u32[]{:S(2)}) collective-permute-start(bf16[256,128]{1,0:T(8,128)(2,1)S(1)} %fusion.3), channel_id=1, source_target_pairs={{0,8},{8,0},{1,9},{9,1},{2,10},{10,2},{3,11},{11,3},{4,12},{12,4},... | collective-permute-start | bytes 196616 | tf_op jit(solution)/shard_map/ppermute | solution.py:253
  82.0 17.0 %all-to-all-start.1 = ((bf16[16,128,128]{2,1,0:T(8,128)(2,1)}), bf16[16,128,128]{2,1,0:T(8,128)(2,1)S(1)}, u32[]{:S(2)}, u32[]{:S(2)}) async-start(bf16[16,128,128]{2,1,0:T(8,128)(2,1)} %add_convert_fusion), calls=%async_computation.1 | async-start | bytes 1048576 | tf_op jit(solution)/shard_map/all_to_all | solution.py:251

commit v3 on v1

v3 whole, which is shorter than its diff:
```python
import math

import jax
import jax.numpy as jnp
import numpy as np
from jax import lax
from jax.experimental import pallas as pl
from jax.experimental.pallas import tpu as pltpu
from jax.sharding import Mesh, PartitionSpec as P

AXES = ("z", "yh", "c", "x", "yl")
SIZES = (8, 2, 2, 4, 2)
PLANE = ("yh", "x", "yl")
ROWS = 128
WIDTH = 128
NDOCS = 16
TILE = 2048
RUN = 1024
CHUNK = 256
PACK = 272
LOG2E = math.log2(math.e)
SCALE = 128.0 ** -0.5
BF = jnp.bfloat16
F32 = jnp.float32
ONE = jax.ShapeDtypeStruct((2 * ROWS, WIDTH), BF)
TWO = jax.ShapeDtypeStruct((2, 2 * ROWS, WIDTH), BF)


def pairs_along_z(k, both_ways, back):
    pairs = []
    for i in range(256):
        z, yh, c, x, yl = (int(v) for v in np.unravel_index(i, SIZES))
        t = z - k + 8 if both_ways and c == 1 else z + k
        if z < t < 8:
            j = int(np.ravel_multi_index((t, yh, c, x, yl), SIZES))
            pairs.append((j, i) if back else (i, j))
    return pairs


def call(body, out_shape, *args, smem=0, scratch=()):
    specs = [pl.BlockSpec(memory_space=pltpu.SMEM)] * smem
    specs += [pl.BlockSpec(memory_space=pltpu.VMEM)] * (len(args) - smem)
    return pl.pallas_call(
        body,
        out_shape=out_shape,
        in_specs=specs,
        scratch_shapes=scratch,
        compiler_params=pltpu.CompilerParams(vmem_limit_bytes=32 * 1024 * 1024),
    )(*args)


def split3(x):
    a = x.astype(BF)
    r = x - a.astype(F32)
    b = r.astype(BF)
    c = (r - b.astype(F32)).astype(BF)
    return a, b, c


def pack_kernel(q_ref, g_ref, o_ref, lse_ref, out_ref):
    prod = g_ref[...].astype(F32) * o_ref[...].astype(F32)
    delta = jnp.sum(prod.T, axis=0, keepdims=True)
    lse2 = lse_ref[...] * LOG2E
    parts = split3(lse2) + split3(delta)
    stats = jnp.concatenate(
        [p.astype(F32) for p in parts] + [jnp.zeros((10, ROWS), F32)], axis=0
    ).astype(BF)
    for n in range(16):
        out_ref[n, 0:128] = q_ref[...]
        out_ref[n, 128:256] = g_ref[...]
        out_ref[n, 256:272] = stats


def grad_kernel(
    where_ref, len_ref, allow_ref, qg_ref,
    own_ref, own_x_ref, m1_ref, m2_ref, m3_ref, m4_ref, x1_ref, x2_ref, x3_ref, x4_ref,
    dq_ref, d0_ref, d1_ref, d2_ref, d3_ref, d4_ref, dx_ref,
    k_s, v_s, d_s, dk_acc, dv_acc, dqt_acc, stat_s, start_s, zk_s, ck_s,
):
    z, yh, c, koff = where_ref[0], where_ref[1], where_ref[2], where_ref[3]
    ends = []
    total = jnp.int32(0)
    for d in range(NDOCS):
        total = total + len_ref[d]
        ends.append(total)

    slots = (
        ((own_ref, None), (own_x_ref, None)),
        ((m1_ref, 0), (m1_ref, 1)),
        ((m2_ref, 0), (m2_ref, 1)),
        ((m3_ref, 0), (m3_ref, 1)),
        ((m4_ref, None), (x4_ref, None)),
        ((x1_ref, 0), (x1_ref, 1)),
        ((x2_ref, 0), (x2_ref, 1)),
        ((x3_ref, 0), (x3_ref, 1)),
    )
    for s, halves in enumerate(slots):
        for half, (ref, i) in enumerate(halves):
            rows = slice(half * ROWS, (half + 1) * ROWS)
            k_s[s, rows] = ref[0:128] if i is None else ref[i, 0:128]
            v_s[s, rows] = ref[128:256] if i is None else ref[i, 128:256]
    zk_s[0] = z
    zk_s[4] = z - 4
    for k in range(1, 4):
        zk_s[k] = jnp.where(c == 0, z - k, z + k - 8)
        zk_s[4 + k] = jnp.where(c == 0, z + k - 8, z - k)
    for s in range(8):
        ck_s[s] = c if s < 5 else 1 - c
    dqt_acc[...] = jnp.zeros_like(dqt_acc)

    lane = lax.broadcasted_iota(jnp.int32, (1, RUN), 1)
    for t in range(2):
        st = jnp.concatenate(
            [qg_ref[8 * t + n, 256:272].astype(F32) for n in range(8)], axis=1
        )
        stat_s[t, 0:1] = st[0:1] + st[1:2] + st[2:3]
        stat_s[t, 1:2] = st[3:4] + st[4:5] + st[5:6]
        pos = z * (2 * TILE) + t * TILE + c * RUN + lane
        start = jnp.zeros_like(pos)
        for e in ends:
            start = jnp.where(pos >= e, e, start)
        start_s[t, 0:1] = start

    first = []
    for t in range(2):
        p0 = z * (2 * TILE) + t * TILE + c * RUN
        s0 = jnp.int32(0)
        for e in ends:
            s0 = jnp.where(e <= p0, e, s0)
        first.append((p0, s0))

    row = lax.broadcasted_iota(jnp.int32, (ROWS, 1), 0)

    def slot_step(s, carry):
        zk, ck = zk_s[s], ck_s[s]
        b0 = zk * (2 * TILE) + yh * TILE + ck * RUN + koff
        b1 = zk * (2 * TILE) + yh * TILE + (1 - ck) * RUN + koff
        low, high = jnp.minimum(b0, b1), jnp.maximum(b0, b1)
        dk_acc[...] = jnp.zeros_like(dk_acc)
        dv_acc[...] = jnp.zeros_like(dv_acc)
        for t in range(2):
            p0, s0 = first[t]
            ok = allow_ref[2 * z + t, jnp.maximum(2 * zk + yh, 0)] == 1

            @pl.when(ok & (zk >= 0) & (low <= p0 + RUN - 1) & (high + ROWS - 1 >= s0))
            def _unit():
                k = k_s[s]
                v = v_s[s]
                kt = k.T
                key = jnp.concatenate([b0 + row, b1 + row], axis=0)
                dk = dk_acc[...]
                dv = dv_acc[...]
                for n in range(RUN // CHUNK):
                    cols = slice(n * CHUNK, (n + 1) * CHUNK)
                    blk = 8 * t + 2 * n
                    q = qg_ref[blk : blk + 2, 0:128, :].reshape(CHUNK, WIDTH)
                    g = qg_ref[blk : blk + 2, 128:256, :].reshape(CHUNK, WIDTH)
                    lse2 = stat_s[t, 0:1, cols]
                    delta = stat_s[t, 1:2, cols]
                    sc = lax.dot_general(
                        k, q, (((1,), (1,)), ((), ())), preferred_element_type=F32
                    )
                    dp = lax.dot_general(
                        v, g, (((1,), (1,)), ((), ())), preferred_element_type=F32
                    )
                    vis = (key >= start_s[t, 0:1, cols]) & (key <= p0 + lane[:, cols])
                    p = jnp.where(vis, jnp.exp2(sc * (SCALE * LOG2E) - lse2), 0.0)
                    pb = p.astype(BF)
                    ds = (p * (dp - delta)).astype(BF)
                    dv = dv + jnp.dot(pb, g, preferred_element_type=F32)
                    dk = dk + jnp.dot(ds, q, preferred_element_type=F32)
                    dqt_acc[t, :, cols] += jnp.dot(kt, ds, preferred_element_type=F32)
                dk_acc[...] = dk
                dv_acc[...] = dv

        for half in range(2):
            rows = slice(half * ROWS, (half + 1) * ROWS)
            d_s[2 * s + half, 0:128] = dk_acc[rows].astype(BF)
            d_s[2 * s + half, 128:256] = dv_acc[rows].astype(BF)
        return carry

    lax.fori_loop(0, 8, slot_step, 0)

    for t in range(2):
        for n in range(8):
            dq_ref[8 * t + n] = dqt_acc[t, :, n * ROWS : (n + 1) * ROWS].astype(BF)
    d0_ref[...] = d_s[0]
    d4_ref[...] = d_s[8]
    for k, out in enumerate((d1_ref, d2_ref, d3_ref)):
        out[...] = d_s[2 + 2 * k : 4 + 2 * k]
    dx_ref[0:6] = d_s[10:16]
    dx_ref[6] = d_s[1]
    dx_ref[7] = d_s[9]


def grads(*args):
    return call(
        grad_kernel,
        (
            jax.ShapeDtypeStruct((16, WIDTH, ROWS), BF),
            ONE, TWO, TWO, TWO, ONE,
            jax.ShapeDtypeStruct((8, 2 * ROWS, WIDTH), BF),
        ),
        *args,
        smem=3,
        scratch=[
            pltpu.VMEM((8, CHUNK, WIDTH), BF),
            pltpu.VMEM((8, CHUNK, WIDTH), BF),
            pltpu.VMEM((16, 2 * ROWS, WIDTH), BF),
            pltpu.VMEM((CHUNK, WIDTH), F32),
            pltpu.VMEM((CHUNK, WIDTH), F32),
            pltpu.VMEM((2, WIDTH, RUN), F32),
            pltpu.VMEM((2, 8, RUN), F32),
            pltpu.VMEM((2, 8, RUN), jnp.int32),
            pltpu.SMEM((8,), jnp.int32),
            pltpu.SMEM((8,), jnp.int32),
        ],
    )


def pair_kernel(d0, d1, d2, d3, d4, got, s0, s1, s2, s3, s4):
    for k, (a, out) in enumerate(((d1, s1), (d2, s2), (d3, s3))):
        out[...] = (a[...].astype(F32) + got[2 * k : 2 * k + 2].astype(F32)).astype(BF)
    s0[...] = (d0[...].astype(F32) + got[6].astype(F32)).astype(BF)
    s4[...] = (d4[...].astype(F32) + got[7].astype(F32)).astype(BF)


def column_kernel(s0, e1, e2, e3, e4, keep, send):
    total = e1[...].astype(F32) + e2[...].astype(F32) + e3[...].astype(F32)
    keep[...] = total[0] + e4[...].astype(F32) + s0[...].astype(F32)
    send[...] = total[1].astype(BF)


def last_kernel(dq_all, keep, got, dq_ref, dk_ref, dv_ref):
    dq = dq_all[0].astype(F32)
    for n in range(1, 16):
        dq = dq + dq_all[n].astype(F32)
    dq_ref[...] = (dq.T * SCALE).astype(BF)
    dkv = keep[...] + got[...].astype(F32)
    dk_ref[...] = (dkv[:ROWS] * SCALE).astype(BF)
    dv_ref[...] = dkv[ROWS:].astype(BF)


def on_device(
    queries, key_rows, value_rows, outputs, out_grad, log_sums, doc_lengths, tile_allowed
):
    z, yh, c = lax.axis_index("z"), lax.axis_index("yh"), lax.axis_index("c")
    koff = (lax.axis_index("x") * 2 + lax.axis_index("yl")) * ROWS
    where = jnp.stack([z, yh, c, koff]).astype(jnp.int32)

    def swap(x):
        return lax.ppermute(x, "c", [(0, 1), (1, 0)])

    def along_z(x, k, both_ways=True, back=False):
        return lax.ppermute(x, AXES, pairs_along_z(k, both_ways, back))

    packed = call(
        pack_kernel,
        jax.ShapeDtypeStruct((16, PACK, WIDTH), BF),
        queries, out_grad, outputs, log_sums.reshape(1, ROWS),
    )
    qg = lax.all_to_all(packed, PLANE, 0, 0, tiled=True)

    own = jnp.concatenate([key_rows, value_rows], axis=0)
    own_x = swap(own)
    both = jnp.stack([own, own_x])
    mine = [along_z(both, k) for k in (1, 2, 3)] + [along_z(own, 4, both_ways=False)]
    theirs = [swap(m) for m in mine]

    dq, d0, d1, d2, d3, d4, dx = grads(
        where, doc_lengths, tile_allowed, qg, own, own_x, *mine, *theirs
    )
    dq_all = lax.all_to_all(dq, PLANE, 0, 0, tiled=True)
    s0, s1, s2, s3, s4 = call(
        pair_kernel, (ONE, TWO, TWO, TWO, ONE), d0, d1, d2, d3, d4, swap(dx)
    )
    e1, e2, e3 = (along_z(s, k, back=True) for k, s in ((1, s1), (2, s2), (3, s3)))
    e4 = along_z(s4, 4, both_ways=False, back=True)
    keep, send = call(
        column_kernel,
        (jax.ShapeDtypeStruct((2 * ROWS, WIDTH), F32), ONE),
        s0, e1, e2, e3, e4,
    )
    out = jax.ShapeDtypeStruct((ROWS, WIDTH), BF)
    return call(last_kernel, (out, out, out), dq_all, keep, swap(send))


def solution(mesh):
    fine = Mesh(mesh.devices.reshape(SIZES), AXES)
    rows, vec = P(AXES, None), P(AXES)
    return jax.shard_map(
        on_device,
        mesh=fine,
        in_specs=(rows, rows, rows, rows, rows, vec, P(), P()),
        out_specs=(rows, rows, rows),
        check_vma=False,
    )
```

time: 102 us -> 75.2 us (0.74)
  the two profiles are of different devices: /device:TPU:8 before, /device:TPU:32 now
where the time goes in v3:
time: 75.2 us; the launch traced here: 73.7 us
  starting transfers between devices  36.6 us (49%)
  waiting for transfers between devices  25.5 us (34%)
  Pallas kernels  7.73 us (10%)
  local copies, waits for them, and re-layouts  2.95 us (4%)
  between operations  0.86 us (1%)
    ppermute x8, waiting for transfers between devices, along_z(): return lax.ppermute(x, AXES, pairs_along_z(k, both_ways, back))  22.2 us
    ppermute x8, starting transfers between devices, along_z(): return lax.ppermute(x, AXES, pairs_along_z(k, both_ways, back))  22 us
    pallas_call x5, Pallas kernels, call(): pl.pallas_call(body, out_shape=out_shape, in_specs=specs, scratch_shapes=...  7.73 us
    all_to_all x1, starting transfers between devices, on_device(): qg = lax.all_to_all(packed, PLANE, 0, 0, tiled=True)  7.18 us
    all_to_all x1, starting transfers between devices, on_device(): dq_all = lax.all_to_all(dq, PLANE, 0, 0, tiled=True)  6.06 us
    ppermute x7, waiting for transfers between devices, swap(): return lax.ppermute(x, 'c', [(0, 1), (1, 0)])  3.33 us
    unnamed x17, local copies, waits for them, and re-layouts  2.94 us
  transfers between devices with their start and end apart: 17, of which 6 were waited for; matrix products, arithmetic and copies ran while one was open for 0% of the time, Pallas kernels for 0%

profile of v3, /device:TPU:32, one launch (start us, length us, event | category | flops | bytes accessed | tf_op | source)
XLA Modules:
  0.0 73.7 jit_solution(14975670973652217852)
XLA Ops:
  0.6 0.0 copy-start
  0.6 0.7 %copy-done = bf16[128,128]{1,0:T(8,128)(2,1)S(1)} copy-done((bf16[128,128]{1,0:T(8,128)(2,1)S(1)}, bf16[128,128]{1,0:T(8,128)(2,1)}, u32[]{:S(2)}) %copy-start) | copy-done | bytes 32792
  1.4 0.0 copy-start.1
  1.4 0.8 %copy-done.1 = bf16[128,128]{1,0:T(8,128)(2,1)S(1)} copy-done((bf16[128,128]{1,0:T(8,128)(2,1)S(1)}, bf16[128,128]{1,0:T(8,128)(2,1)}, u32[]{:S(2)}) %copy-start.1) | copy-done | bytes 32792
  2.1 0.0 copy-start.2
  2.2 0.8 %copy-done.2 = bf16[128,128]{1,0:T(8,128)(2,1)S(1)} copy-done((bf16[128,128]{1,0:T(8,128)(2,1)S(1)}, bf16[128,128]{1,0:T(8,128)(2,1)}, u32[]{:S(2)}) %copy-start.2) | copy-done | bytes 32792
  2.9 0.0 copy-start.4
  2.9 0.7 copy-done.4
  3.6 1.2 %shard_map.103 = bf16[16,272,128]{2,1,0:T(8,128)(2,1)} custom-call(bf16[128,128]{1,0:T(8,128)(2,1)S(1)} %copy-done, bf16[128,128]{1,0:T(8,128)(2,1)S(1)} %copy-done.1, bf16[128,128]{1,0:T(8,128)(2,1)S(1)} %copy-done.2, f32[1,128]{1,0:T(1,128)S(1)} %bitcast.9), custom_call_target="tpu_custom_call" | custom-call | tf_op jit(solution)/shard_map/pallas_call | solution.py:43
  4.7 0.0 copy-start.6
  4.7 0.0 copy-start.7
  4.7 0.0 copy-start.3
  4.7 0.0 copy-start.5
  4.7 7.2 %all-to-all-start = ((bf16[16,272,128]{2,1,0:T(8,128)(2,1)}), bf16[16,272,128]{2,1,0:T(8,128)(2,1)S(1)}, u32[]{:S(2)}, u32[]{:S(2)}) async-start(bf16[16,272,128]{2,1,0:T(8,128)(2,1)} %shard_map.103), calls=%async_computation | async-start | bytes 2228224 | tf_op jit(solution)/shard_map/all_to_all | solution.py:262
  11.9 0.0 copy-done.6
  11.9 0.0 copy-done.7
  12.0 0.1 collective-permute-start
  12.1 1.2 %collective-permute-done.own_x_ref = bf16[256,128]{1,0:T(8,128)(2,1)S(1)} collective-permute-done((bf16[256,128]{1,0:T(8,128)(2,1)S(1)}, bf16[256,128]{1,0:T(8,128)(2,1)S(1)}, u32[]{:S(2)}, u32[]{:S(2)}) %collective-permute-start) | collective-permute-done | bytes 65568 | tf_op jit(solution)/shard_map/ppermute | solution.py:252
  13.3 7.7 %collective-permute-start.3 = (bf16[2,256,128]{2,1,0:T(8,128)(2,1)S(1)}, bf16[2,256,128]{2,1,0:T(8,128)(2,1)S(1)}, u32[]{:S(2)}, u32[]{:S(2)}) collective-permute-start(bf16[2,256,128]{2,1,0:T(8,128)(2,1)S(1)} %pad_maximum_fusion), channel_id=1, source_target_pairs={{0,96},{1,97},{2,98},{3,99},{4,100},{5,101},{6,102},{7,103},{8,168... | collective-permute-start | bytes 393224 | tf_op jit(solution)/shard_map/ppermute | solution.py:255
  21.1 3.4 %collective-permute-start.2 = (bf16[2,256,128]{2,1,0:T(8,128)(2,1)S(1)}, bf16[2,256,128]{2,1,0:T(8,128)(2,1)S(1)}, u32[]{:S(2)}, u32[]{:S(2)}) collective-permute-start(bf16[2,256,128]{2,1,0:T(8,128)(2,1)S(1)} %pad_maximum_fusion), channel_id=1, source_target_pairs={{0,64},{1,65},{2,66},{3,67},{4,68},{5,69},{6,70},{7,71},{8,200},{9... | collective-permute-start | bytes 393224 | tf_op jit(solution)/shard_map/ppermute | solution.py:255
  24.5 2.9 %collective-permute-start.1 = (bf16[2,256,128]{2,1,0:T(8,128)(2,1)S(1)}, bf16[2,256,128]{2,1,0:T(8,128)(2,1)S(1)}, u32[]{:S(2)}, u32[]{:S(2)}) collective-permute-start(bf16[2,256,128]{2,1,0:T(8,128)(2,1)S(1)} %pad_maximum_fusion), channel_id=1, source_target_pairs={{0,32},{1,33},{2,34},{3,35},{4,36},{5,37},{6,38},{7,39},{8,232},{9... | collective-permute-start | bytes 393224 | tf_op jit(solution)/shard_map/ppermute | solution.py:255
  27.4 1.3 %collective-permute-start.4 = (bf16[256,128]{1,0:T(8,128)(2,1)S(1)}, bf16[256,128]{1,0:T(8,128)(2,1)S(1)}, u32[]{:S(2)}, u32[]{:S(2)}) collective-permute-start(bf16[256,128]{1,0:T(8,128)(2,1)S(1)} %constant_dynamic-update-slice_fusion.own_ref), channel_id=1, source_target_pairs={{0,128},{1,129},{2,130},{3,131},{4,132},{5,133},{6,134},{7,135},{8... | collective-permute-start | bytes 196616 | tf_op jit(solution)/shard_map/ppermute | solution.py:255
  28.7 0.0 collective-permute-done.3.m3_ref
  28.7 0.1 collective-permute-start.7
  28.8 0.3 collective-permute-done.2.m2_ref
  29.1 0.2 collective-permute-start.6
  29.3 2.0 %collective-permute-done.1.m1_ref = bf16[2,256,128]{2,1,0:T(8,128)(2,1)S(1)} collective-permute-done((bf16[2,256,128]{2,1,0:T(8,128)(2,1)S(1)}, bf16[2,256,128]{2,1,0:T(8,128)(2,1)S(1)}, u32[]{:S(2)}, u32[]{:S(2)}) %collective-permute-start.1) | collective-permute-done | bytes 131104 | tf_op jit(solution)/shard_map/ppermute | solution.py:255
  31.3 0.0 collective-permute-start.5
  31.3 0.0 collective-permute-done.4.m4_ref
  31.3 0.5 collective-permute-start.8
  31.8 0.1 pad_add_fusion.where_ref
  31.9 0.9 %collective-permute-done.8.x4_ref = bf16[256,128]{1,0:T(8,128)(2,1)S(1)} collective-permute-done((bf16[256,128]{1,0:T(8,128)(2,1)S(1)}, bf16[256,128]{1,0:T(8,128)(2,1)S(1)}, u32[]{:S(2)}, u32[]{:S(2)}) %collective-permute-start.8) | collective-permute-done | bytes 65568 | tf_op jit(solution)/shard_map/ppermute | solution.py:252
  32.8 0.0 collective-permute-done.7.x3_ref
  32.8 0.0 collective-permute-done.6.x2_ref
  32.8 0.0 collective-permute-done.5.x1_ref
  32.8 0.0 all-to-all-done.qg_ref
  32.8 0.0 copy-done.3
  32.8 0.0 copy-done.5
  32.8 5.6 %shard_map.104 = (bf16[16,128,128]{2,1,0:T(8,128)(2,1)}, bf16[256,128]{1,0:T(8,128)(2,1)S(1)}, bf16[2,256,128]{2,1,0:T(8,128)(2,1)S(1)}, bf16[2,256,128]{2,1,0:T...) custom-call(s32[4]{0:T(128)S(1)} %pad_add_fusion.where_ref, ...), custom_call_target="tpu_custom_call" | custom-call | tf_op jit(solution)/shard_map/pallas_call | solution.py:43
  38.4 0.3 collective-permute-start.9
  38.8 6.1 %all-to-all-start.1 = ((bf16[16,128,128]{2,1,0:T(8,128)(2,1)}), bf16[16,128,128]{2,1,0:T(8,128)(2,1)S(1)}, u32[]{:S(2)}, u32[]{:S(2)}) async-start(bf16[16,128,128]{2,1,0:T(8,128)(2,1)} %get-tuple-element.17), calls=%async_computation.1 | async-start | bytes 1048576 | tf_op jit(solution)/shard_map/all_to_all | solution.py:273
  44.8 0.0 collective-permute-done.9.got
  44.8 0.1 shard_map.105
  45.0 2.8 %collective-permute-start.10 = (bf16[2,256,128]{2,1,0:T(8,128)(2,1)S(1)}, bf16[2,256,128]{2,1,0:T(8,128)(2,1)S(1)}, u32[]{:S(2)}, u32[]{:S(2)}) collective-permute-start(bf16[2,256,128]{2,1,0:T(8,128)(2,1)S(1)} %get-tuple-element.25), channel_id=1, source_target_pairs={{32,0},{33,1},{34,2},{35,3},{36,4},{37,5},{38,6},{39,7},{232,8},{2... | collective-permute-start | bytes 393224 | tf_op jit(solution)/shard_map/ppermute | solution.py:255
  47.8 1.3 %collective-permute-start.11 = (bf16[2,256,128]{2,1,0:T(8,128)(2,1)S(1)}, bf16[2,256,128]{2,1,0:T(8,128)(2,1)S(1)}, u32[]{:S(2)}, u32[]{:S(2)}) collective-permute-start(bf16[2,256,128]{2,1,0:T(8,128)(2,1)S(1)} %get-tuple-element.26), channel_id=1, source_target_pairs={{64,0},{65,1},{66,2},{67,3},{68,4},{69,5},{70,6},{71,7},{200,8},{2... | collective-permute-start | bytes 393224 | tf_op jit(solution)/shard_map/ppermute | solution.py:255
  49.1 1.3 %collective-permute-start.12 = (bf16[2,256,128]{2,1,0:T(8,128)(2,1)S(1)}, bf16[2,256,128]{2,1,0:T(8,128)(2,1)S(1)}, u32[]{:S(2)}, u32[]{:S(2)}) collective-permute-start(bf16[2,256,128]{2,1,0:T(8,128)(2,1)S(1)} %get-tuple-element.27), channel_id=1, source_target_pairs={{96,0},{97,1},{98,2},{99,3},{100,4},{101,5},{102,6},{103,7},{168,8... | collective-permute-start | bytes 393224 | tf_op jit(solution)/shard_map/ppermute | solution.py:255
  50.4 1.3 %collective-permute-start.13 = (bf16[256,128]{1,0:T(8,128)(2,1)S(1)}, bf16[256,128]{1,0:T(8,128)(2,1)S(1)}, u32[]{:S(2)}, u32[]{:S(2)}) collective-permute-start(bf16[256,128]{1,0:T(8,128)(2,1)S(1)} %get-tuple-element.28), channel_id=1, source_target_pairs={{128,0},{129,1},{130,2},{131,3},{132,4},{133,5},{134,6},{135,7},{1... | collective-permute-start | bytes 196616 | tf_op jit(solution)/shard_map/ppermute | solution.py:255
  51.7 19.9 %collective-permute-done.13.e4 = bf16[256,128]{1,0:T(8,128)(2,1)S(1)} collective-permute-done((bf16[256,128]{1,0:T(8,128)(2,1)S(1)}, bf16[256,128]{1,0:T(8,128)(2,1)S(1)}, u32[]{:S(2)}, u32[]{:S(2)}) %collective-permute-start.13) | collective-permute-done | bytes 65568 | tf_op jit(solution)/shard_map/ppermute | solution.py:255
  71.5 0.0 collective-permute-done.10.e1
  71.5 0.0 collective-permute-done.11.e2
  71.5 0.0 collective-permute-done.12.e3
  71.5 0.1 shard_map.106
  71.6 0.1 collective-permute-start.14
  71.7 0.0 all-to-all-done.1.dq_all
  71.7 1.2 %collective-permute-done.14.got = bf16[256,128]{1,0:T(8,128)(2,1)S(1)} collective-permute-done((bf16[256,128]{1,0:T(8,128)(2,1)S(1)}, bf16[256,128]{1,0:T(8,128)(2,1)S(1)}, u32[]{:S(2)}, u32[]{:S(2)}) %collective-permute-start.14) | collective-permute-done | bytes 65568 | tf_op jit(solution)/shard_map/ppermute | solution.py:252
  73.0 0.8 %shard_map.107 = (bf16[128,128]{1,0:T(8,128)(2,1)}, bf16[128,128]{1,0:T(8,128)(2,1)}, bf16[128,128]{1,0:T(8,128)(2,1)}) custom-call(bf16[16,128,128]{2,1,0:T(8,128)(2,1)S(1)} %all-to-all-done.1.dq_all, f32[256,128]{1,0:T(8,128)S(1)} %get-tuple-element.29.keep, bf16[256,128]{1,0:T(8,128)(2,1)S(1)} %collective-permute-done.14.got), custom_call_target="tpu_custom_call" | custom-call | tf_op jit(solution)/shard_map/pallas_call | solution.py:43
  (3 shorter events, 0.0 us)
Async XLA Ops:
  0.6 0.8 %copy-start = (bf16[128,128]{1,0:T(8,128)(2,1)S(1)}, bf16[128,128]{1,0:T(8,128)(2,1)}, u32[]{:S(2)}) copy-start(bf16[128,128]{1,0:T(8,128)(2,1)} %q_ref.1) | copy-start | bytes 98308
  1.4 0.8 %copy-start.1 = (bf16[128,128]{1,0:T(8,128)(2,1)S(1)}, bf16[128,128]{1,0:T(8,128)(2,1)}, u32[]{:S(2)}) copy-start(bf16[128,128]{1,0:T(8,128)(2,1)} %g_ref.1) | copy-start | bytes 98308
  2.1 0.8 %copy-start.2 = (bf16[128,128]{1,0:T(8,128)(2,1)S(1)}, bf16[128,128]{1,0:T(8,128)(2,1)}, u32[]{:S(2)}) copy-start(bf16[128,128]{1,0:T(8,128)(2,1)} %o_ref.1) | copy-start | bytes 98308
  2.9 0.7 copy-start.4
  4.7 7.2 %copy-start.6 = (bf16[128,128]{1,0:T(8,128)(2,1)S(1)}, bf16[128,128]{1,0:T(8,128)(2,1)}, u32[]{:S(2)}) copy-start(bf16[128,128]{1,0:T(8,128)(2,1)} %param.9) | copy-start | bytes 98308
  4.7 7.2 %copy-start.7 = (bf16[128,128]{1,0:T(8,128)(2,1)S(1)}, bf16[128,128]{1,0:T(8,128)(2,1)}, u32[]{:S(2)}) copy-start(bf16[128,128]{1,0:T(8,128)(2,1)} %param.10) | copy-start | bytes 98308
  4.7 28.1 %copy-start.3 = (s32[16,16]{1,0:T(8,128)S(1)}, s32[16,16]{1,0:T(8,128)}, u32[]{:S(2)}) copy-start(s32[16,16]{1,0:T(8,128)} %allow_ref.1) | copy-start | bytes 3076
  4.7 28.1 %copy-start.5 = (s32[16]{0:T(128)S(1)}, s32[16]{0:T(128)}, u32[]{:S(2)}) copy-start(s32[16]{0:T(128)} %len_ref.1) | copy-start | bytes 196
  4.7 28.1 %all-to-all-start = ((bf16[16,272,128]{2,1,0:T(8,128)(2,1)}), bf16[16,272,128]{2,1,0:T(8,128)(2,1)S(1)}, u32[]{:S(2)}, u32[]{:S(2)}) async-start(bf16[16,272,128]{2,1,0:T(8,128)(2,1)} %shard_map.103), calls=%async_computation | async-start | bytes 2228224 | tf_op jit(solution)/shard_map/all_to_all | solution.py:262
  12.0 1.3 %collective-permute-start = (bf16[256,128]{1,0:T(8,128)(2,1)S(1)}, bf16[256,128]{1,0:T(8,128)(2,1)S(1)}, u32[]{:S(2)}, u32[]{:S(2)}) collective-permute-start(bf16[256,128]{1,0:T(8,128)(2,1)S(1)} %constant_dynamic-update-slice_fusion.own_ref), channel_id=1, source_target_pairs={{0,8},{8,0},{1,9},{9,1},{2,10},{10,2},{3,11},{11,3},{4,12},{12,4},... | collective-permute-start | bytes 196616 | tf_op jit(solution)/shard_map/ppermute | solution.py:252
  13.3 15.4 %collective-permute-start.3 = (bf16[2,256,128]{2,1,0:T(8,128)(2,1)S(1)}, bf16[2,256,128]{2,1,0:T(8,128)(2,1)S(1)}, u32[]{:S(2)}, u32[]{:S(2)}) collective-permute-start(bf16[2,256,128]{2,1,0:T(8,128)(2,1)S(1)} %pad_maximum_fusion), channel_id=1, source_target_pairs={{0,96},{1,97},{2,98},{3,99},{4,100},{5,101},{6,102},{7,103},{8,168... | collective-permute-start | bytes 393224 | tf_op jit(solution)/shard_map/ppermute | solution.py:255
  21.1 8.0 %collective-permute-start.2 = (bf16[2,256,128]{2,1,0:T(8,128)(2,1)S(1)}, bf16[2,256,128]{2,1,0:T(8,128)(2,1)S(1)}, u32[]{:S(2)}, u32[]{:S(2)}) collective-permute-start(bf16[2,256,128]{2,1,0:T(8,128)(2,1)S(1)} %pad_maximum_fusion), channel_id=1, source_target_pairs={{0,64},{1,65},{2,66},{3,67},{4,68},{5,69},{6,70},{7,71},{8,200},{9... | collective-permute-start | bytes 393224 | tf_op jit(solution)/shard_map/ppermute | solution.py:255
  24.5 6.9 %collective-permute-start.1 = (bf16[2,256,128]{2,1,0:T(8,128)(2,1)S(1)}, bf16[2,256,128]{2,1,0:T(8,128)(2,1)S(1)}, u32[]{:S(2)}, u32[]{:S(2)}) collective-permute-start(bf16[2,256,128]{2,1,0:T(8,128)(2,1)S(1)} %pad_maximum_fusion), channel_id=1, source_target_pairs={{0,32},{1,33},{2,34},{3,35},{4,36},{5,37},{6,38},{7,39},{8,232},{9... | collective-permute-start | bytes 393224 | tf_op jit(solution)/shard_map/ppermute | solution.py:255
  27.4 3.9 %collective-permute-start.4 = (bf16[256,128]{1,0:T(8,128)(2,1)S(1)}, bf16[256,128]{1,0:T(8,128)(2,1)S(1)}, u32[]{:S(2)}, u32[]{:S(2)}) collective-permute-start(bf16[256,128]{1,0:T(8,128)(2,1)S(1)} %constant_dynamic-update-slice_fusion.own_ref), channel_id=1, source_target_pairs={{0,128},{1,129},{2,130},{3,131},{4,132},{5,133},{6,134},{7,135},{8... | collective-permute-start | bytes 196616 | tf_op jit(solution)/shard_map/ppermute | solution.py:255
  28.7 4.1 %collective-permute-start.7 = (bf16[2,256,128]{2,1,0:T(8,128)(2,1)S(1)}, bf16[2,256,128]{2,1,0:T(8,128)(2,1)S(1)}, u32[]{:S(2)}, u32[]{:S(2)}) collective-permute-start(bf16[2,256,128]{2,1,0:T(8,128)(2,1)S(1)} %collective-permute-done.3.m3_ref), channel_id=1, source_target_pairs={{0,8},{8,0},{1,9},{9,1},{2,10},{10,2},{3,11},{11,3},{4,12},{12,4},... | collective-permute-start | bytes 393224 | tf_op jit(solution)/shard_map/ppermute | solution.py:252
  29.1 3.7 %collective-permute-start.6 = (bf16[2,256,128]{2,1,0:T(8,128)(2,1)S(1)}, bf16[2,256,128]{2,1,0:T(8,128)(2,1)S(1)}, u32[]{:S(2)}, u32[]{:S(2)}) collective-permute-start(bf16[2,256,128]{2,1,0:T(8,128)(2,1)S(1)} %collective-permute-done.2.m2_ref), channel_id=1, source_target_pairs={{0,8},{8,0},{1,9},{9,1},{2,10},{10,2},{3,11},{11,3},{4,12},{12,4},... | collective-permute-start | bytes 393224 | tf_op jit(solution)/shard_map/ppermute | solution.py:252
  31.3 1.5 %collective-permute-start.5 = (bf16[2,256,128]{2,1,0:T(8,128)(2,1)S(1)}, bf16[2,256,128]{2,1,0:T(8,128)(2,1)S(1)}, u32[]{:S(2)}, u32[]{:S(2)}) collective-permute-start(bf16[2,256,128]{2,1,0:T(8,128)(2,1)S(1)} %collective-permute-done.1.m1_ref), channel_id=1, source_target_pairs={{0,8},{8,0},{1,9},{9,1},{2,10},{10,2},{3,11},{11,3},{4,12},{12,4},... | collective-permute-start | bytes 393224 | tf_op jit(solution)/shard_map/ppermute | solution.py:252
  31.3 1.4 %collective-permute-start.8 = (bf16[256,128]{1,0:T(8,128)(2,1)S(1)}, bf16[256,128]{1,0:T(8,128)(2,1)S(1)}, u32[]{:S(2)}, u32[]{:S(2)}) collective-permute-start(bf16[256,128]{1,0:T(8,128)(2,1)S(1)} %collective-permute-done.4.m4_ref), channel_id=1, source_target_pairs={{0,8},{8,0},{1,9},{9,1},{2,10},{10,2},{3,11},{11,3},{4,12},{12,4},... | collective-permute-start | bytes 196616 | tf_op jit(solution)/shard_map/ppermute | solution.py:252
  38.4 6.4 %collective-permute-start.9 = (bf16[8,256,128]{2,1,0:T(8,128)(2,1)S(1)}, bf16[8,256,128]{2,1,0:T(8,128)(2,1)S(1)}, u32[]{:S(2)}, u32[]{:S(2)}) collective-permute-start(bf16[8,256,128]{2,1,0:T(8,128)(2,1)S(1)} %get-tuple-element.23), channel_id=1, source_target_pairs={{0,8},{8,0},{1,9},{9,1},{2,10},{10,2},{3,11},{11,3},{4,12},{12,4},... | collective-permute-start | bytes 1572872 | tf_op jit(solution)/shard_map/ppermute | solution.py:252
  38.8 33.0 %all-to-all-start.1 = ((bf16[16,128,128]{2,1,0:T(8,128)(2,1)}), bf16[16,128,128]{2,1,0:T(8,128)(2,1)S(1)}, u32[]{:S(2)}, u32[]{:S(2)}) async-start(bf16[16,128,128]{2,1,0:T(8,128)(2,1)} %get-tuple-element.17), calls=%async_computation.1 | async-start | bytes 1048576 | tf_op jit(solution)/shard_map/all_to_all | solution.py:273
  45.0 26.6 %collective-permute-start.10 = (bf16[2,256,128]{2,1,0:T(8,128)(2,1)S(1)}, bf16[2,256,128]{2,1,0:T(8,128)(2,1)S(1)}, u32[]{:S(2)}, u32[]{:S(2)}) collective-permute-start(bf16[2,256,128]{2,1,0:T(8,128)(2,1)S(1)} %get-tuple-element.25), channel_id=1, source_target_pairs={{32,0},{33,1},{34,2},{35,3},{36,4},{37,5},{38,6},{39,7},{232,8},{2... | collective-permute-start | bytes 393224 | tf_op jit(solution)/shard_map/ppermute | solution.py:255
  47.8 23.8 %collective-permute-start.11 = (bf16[2,256,128]{2,1,0:T(8,128)(2,1)S(1)}, bf16[2,256,128]{2,1,0:T(8,128)(2,1)S(1)}, u32[]{:S(2)}, u32[]{:S(2)}) collective-permute-start(bf16[2,256,128]{2,1,0:T(8,128)(2,1)S(1)} %get-tuple-element.26), channel_id=1, source_target_pairs={{64,0},{65,1},{66,2},{67,3},{68,4},{69,5},{70,6},{71,7},{200,8},{2... | collective-permute-start | bytes 393224 | tf_op jit(solution)/shard_map/ppermute | solution.py:255
  49.1 22.5 %collective-permute-start.12 = (bf16[2,256,128]{2,1,0:T(8,128)(2,1)S(1)}, bf16[2,256,128]{2,1,0:T(8,128)(2,1)S(1)}, u32[]{:S(2)}, u32[]{:S(2)}) collective-permute-start(bf16[2,256,128]{2,1,0:T(8,128)(2,1)S(1)} %get-tuple-element.27), channel_id=1, source_target_pairs={{96,0},{97,1},{98,2},{99,3},{100,4},{101,5},{102,6},{103,7},{168,8... | collective-permute-start | bytes 393224 | tf_op jit(solution)/shard_map/ppermute | solution.py:255
  50.4 21.2 %collective-permute-start.13 = (bf16[256,128]{1,0:T(8,128)(2,1)S(1)}, bf16[256,128]{1,0:T(8,128)(2,1)S(1)}, u32[]{:S(2)}, u32[]{:S(2)}) collective-permute-start(bf16[256,128]{1,0:T(8,128)(2,1)S(1)} %get-tuple-element.28), channel_id=1, source_target_pairs={{128,0},{129,1},{130,2},{131,3},{132,4},{133,5},{134,6},{135,7},{1... | collective-permute-start | bytes 196616 | tf_op jit(solution)/shard_map/ppermute | solution.py:255
  71.6 1.3 %collective-permute-start.14 = (bf16[256,128]{1,0:T(8,128)(2,1)S(1)}, bf16[256,128]{1,0:T(8,128)(2,1)S(1)}, u32[]{:S(2)}, u32[]{:S(2)}) collective-permute-start(bf16[256,128]{1,0:T(8,128)(2,1)S(1)} %get-tuple-element.30), channel_id=1, source_target_pairs={{0,8},{8,0},{1,9},{9,1},{2,10},{10,2},{3,11},{11,3},{4,12},{12,4},... | collective-permute-start | bytes 196616 | tf_op jit(solution)/shard_map/ppermute | solution.py:252
